TPU v7x, 32 devices: a whole 2x2x4 slice. The times are simulated.
32 devices in a mesh: wide: 8 (over y, x, core), narrow: 4 (over z).
Axes of the slice: x: 2, y: 2, z: 4, core: 2. Of those that a mesh axis runs over, the one named last changes fastest.
Arguments:
- tokens: bfloat16 [32768, 768], P(('wide', 'narrow')), may hold values from -6 to 6
- doc_lengths: int32 [64, 4], P(('wide', 'narrow')), may hold values from 1 to 256, 512 in all within a row
- cotangent: bfloat16 [32768, 768], P(('wide', 'narrow')), may hold values from -6 to 6
- owners: int32 [12], replicated, may hold values from 0 to 3, as said below
- step_count: int32 [1], replicated, may hold values from 1 to 20
- master: float32 [768, 24, 768], P('wide', 'narrow')
- moment_one: float32 [768, 24, 768], P('wide', 'narrow')
- moment_two: float32 [768, 24, 768], P('wide', 'narrow'), as said below
- vectors: float32 [13, 768], replicated
- vector_one: float32 [13, 768], replicated
- vector_two: float32 [13, 768], replicated, as said below
Outputs:
- layer_out: bfloat16 [32768, 768], P(('wide', 'narrow'))
- input_grad: float32 [32768, 768], P(('wide', 'narrow'))
- grad_norm: float32 [], replicated
- block_grads: float32 [768, 24, 768], P('wide', 'narrow')
- new_master: float32 [768, 24, 768], P('wide', 'narrow')
- new_first: float32 [768, 24, 768], P('wide', 'narrow')
- new_second: float32 [768, 24, 768], P('wide', 'narrow')
- new_copies: bfloat16 [768, 24, 768], P('wide', 'narrow')
- vector_grads: float32 [13, 768], replicated
- new_vectors: float32 [13, 768], replicated
- vector_first: float32 [13, 768], replicated
- vector_second: float32 [13, 768], replicated
Inputs may be any that keep to these rules, and one draw needn't show every extreme that they name: `owners`: each index of narrow owns at most 6 of the 12 blocks, and one owns exactly 6. `doc_lengths`: each row sums to 512; its longest document has exactly 256 tokens. `moment_two`: Positive. `vector_two`: Positive.
All inputs are finite; a program needn't handle non-finite values.
Results may differ from a plain program's by a relative error of at most 0.0098.
Values may be sent and summed in bfloat16 or wider, within the bound.
No kernel may reach another device: no remote copies, remote signals or barrier semaphores. Data moves between devices by JAX's collectives and lax.ppermute only.
A program may use at most 256 MiB of HBM per device.

v0:
```python
from functools import partial

import jax
import jax.numpy as jnp
from jax import lax
from jax.sharding import PartitionSpec as P

D = 768
HEADS = 12
HEAD = 64
ROT = 16
FF = 3072


norm_epsilon = 1e-05
beta_first = 0.5
beta_second = 0.5
adam_epsilon = 1e-08
learn_rate = 0.02
vector_rate = 0.1
weight_decay = 0.1
masked_fill = -1e30
rope_base = 10000.0


def slot_table(owners, capacity):
    number = owners.shape[0]
    order = jnp.arange(number, dtype=jnp.int32)
    before = (owners[:, None] == owners[None, :]) & (order[None, :] < order[:, None])
    return owners * capacity + jnp.sum(before.astype(jnp.int32), axis=1)


def doc_layout(lengths, seq_length):
    ends = jnp.cumsum(lengths, axis=1)
    position = jnp.arange(seq_length, dtype=jnp.int32)
    passed = position[None, :, None] >= ends[:, None, :]
    doc_index = jnp.sum(passed.astype(jnp.int32), axis=2)
    doc_start = jnp.sum(jnp.where(passed, lengths[:, None, :], 0), axis=2)
    visible = (doc_index[:, :, None] == doc_index[:, None, :]) & (
        position[None, :, None] >= position[None, None, :]
    )
    return (visible, position[None, :] - doc_start)


def angles(offsets, rotary):
    half = rotary // 2
    freqs = jnp.power(rope_base, -2.0 * jnp.arange(half, dtype=jnp.float32) / rotary)
    turned = offsets.astype(jnp.float32)[:, :, None] * freqs
    doubled = jnp.concatenate([turned, turned], axis=-1)[:, :, None, :]
    return (jnp.cos(doubled), jnp.sin(doubled))


def rotate(values, cosine, sine_part):
    rotary = cosine.shape[-1]
    half = rotary // 2
    head_part = values[..., :rotary]
    swapped = jnp.concatenate([-head_part[..., half:], head_part[..., :half]], axis=-1)
    return jnp.concatenate(
        [head_part * cosine + swapped * sine_part, values[..., rotary:]], axis=-1
    )


def layer_norms(inputs, vectors):
    centred = inputs - jnp.mean(inputs, axis=-1, keepdims=True)
    scaled = centred * lax.rsqrt(jnp.mean(centred * centred, axis=-1, keepdims=True) + norm_epsilon)
    return (scaled * vectors[0] + vectors[1], scaled * vectors[2] + vectors[3])


def masked_scores(queries, key_low, visible):
    scores = jnp.einsum(
        "sqhd,skhd->shqk", queries, key_low, preferred_element_type=jnp.float32
    ) * HEAD ** (-0.5)
    return jnp.where(visible[:, None], scores, masked_fill)


def adam_update(gradient, weight, moment, square, rate, decay, first_fix, second_fix):
    moment_new = beta_first * moment + (1.0 - beta_first) * gradient
    square_new = beta_second * square + (1.0 - beta_second) * gradient * gradient
    update = moment_new / first_fix / (jnp.sqrt(square_new / second_fix) + adam_epsilon)
    return (weight - rate * (update + decay * weight), moment_new, square_new)


def term_of(inputs, cot_rows, model_width, row_count):
    in_piece = lax.slice_in_dim(inputs, 0, row_count, axis=2)
    product = jnp.einsum("tar,tbc->rabc", in_piece, cot_rows, preferred_element_type=jnp.float32)
    return product.reshape(row_count, inputs.shape[1] * cot_rows.shape[1], model_width)


def per_device(
    tokens,
    doc_lengths,
    cotangent,
    owners,
    step_count,
    master,
    moment_one,
    moment_two,
    vectors,
    vector_one,
    vector_two,
):
    shard_rows, capacity, model_width = master.shape
    seq_count = doc_lengths.shape[0]
    tok_count = tokens.shape[0]
    seq_length = tok_count // seq_count
    spread = FF // D
    block_count = owners.shape[0]
    bounds = ((0, 3), (3, 4), (4, 4 + spread), (4 + spread, block_count))
    narrow_index = lax.axis_index("narrow")
    slot_of = slot_table(owners, capacity)
    copies = lax.all_gather(master.astype(jnp.bfloat16), "narrow", axis=1, tiled=True)
    shards = jnp.take(copies, slot_of, axis=1)

    def forward_weights(shard):
        return lax.all_gather(shard, "wide", axis=0, tiled=True)

    w_qkv, w_out, w_up, w_down = [
        forward_weights(shards[:, begin:finish]) for begin, finish in bounds
    ]
    inputs = tokens.astype(jnp.float32)
    (norm_one, norm_two), norm_back = jax.vjp(layer_norms, inputs, vectors)
    h_one = norm_one.astype(jnp.bfloat16)
    h_two = norm_two.astype(jnp.bfloat16)
    qkv = jnp.einsum("td,dkc->tkc", h_one, w_qkv, preferred_element_type=jnp.float32) + vectors[4:7]
    shaped = qkv.reshape(seq_count, seq_length, 3, HEADS, HEAD)
    visible, offsets = doc_layout(doc_lengths, seq_length)
    cosine, sine_part = angles(offsets, ROT)

    def turn_pair(query_pre, key_pre):
        return (rotate(query_pre, cosine, sine_part), rotate(key_pre, cosine, sine_part))

    (query_turn, key_turn), turn_back = jax.vjp(turn_pair, shaped[:, :, 0], shaped[:, :, 1])
    queries = query_turn.astype(jnp.bfloat16)
    key_low = key_turn.astype(jnp.bfloat16)
    value_low = shaped[:, :, 2].astype(jnp.bfloat16)
    masked = masked_scores(queries, key_low, visible)
    row_max = jnp.max(masked, axis=-1, keepdims=True)
    shifted = jnp.exp(masked - row_max)
    row_sum = jnp.sum(shifted, axis=-1, keepdims=True)
    prob_low = (shifted / row_sum).astype(jnp.bfloat16)
    log_total = row_max + jnp.log(row_sum)
    mixed = jnp.einsum("shqk,skhd->sqhd", prob_low, value_low, preferred_element_type=jnp.float32)
    attn_in = mixed.reshape(tok_count, model_width).astype(jnp.bfloat16)
    attn_out = (
        jnp.einsum("td,dkc->tc", attn_in, w_out, preferred_element_type=jnp.float32) + vectors[7]
    )
    pre_act = (
        jnp.einsum("td,djc->tjc", h_two, w_up, preferred_element_type=jnp.float32)
        + vectors[8 : 8 + spread]
    )
    act, gelu_back = jax.vjp(partial(jax.nn.gelu, approximate=False), pre_act)
    act_low = act.astype(jnp.bfloat16)
    mlp_out = (
        jnp.einsum("tjr,rjc->tc", act_low, w_down, preferred_element_type=jnp.float32)
        + vectors[8 + spread]
    )
    layer_out = (inputs + attn_out + mlp_out).astype(jnp.bfloat16)

    def backward_weights(shard):
        return lax.all_gather(shard, "wide", axis=0, tiled=True)

    b_qkv, b_out, b_up, b_down = [
        backward_weights(shards[:, begin:finish]) for begin, finish in bounds
    ]
    upstream = cotangent.astype(jnp.float32)
    (d_pre,) = gelu_back(
        jnp.einsum("tc,rjc->tjr", cotangent, b_down, preferred_element_type=jnp.float32)
    )
    d_pre_low = d_pre.astype(jnp.bfloat16)
    d_attn = jnp.einsum("tc,dkc->td", cotangent, b_out, preferred_element_type=jnp.float32).astype(
        jnp.bfloat16
    )
    d_mixed = d_attn.reshape(seq_count, seq_length, HEADS, HEAD)
    prob_back = jnp.exp(masked_scores(queries, key_low, visible) - log_total)
    d_value = jnp.einsum(
        "shqk,sqhd->skhd",
        prob_back.astype(jnp.bfloat16),
        d_mixed,
        preferred_element_type=jnp.float32,
    )
    d_prob = jnp.einsum("sqhd,skhd->shqk", d_mixed, value_low, preferred_element_type=jnp.float32)
    d_score = (prob_back * (d_prob - jnp.sum(d_prob * prob_back, axis=-1, keepdims=True))).astype(
        jnp.bfloat16
    )
    d_query = jnp.einsum(
        "shqk,skhd->sqhd", d_score, key_low, preferred_element_type=jnp.float32
    ) * HEAD ** (-0.5)
    d_key = jnp.einsum(
        "shqk,sqhd->skhd", d_score, queries, preferred_element_type=jnp.float32
    ) * HEAD ** (-0.5)
    d_query_pre, d_key_pre = turn_back((d_query, d_key))
    d_qkv = (
        jnp.stack([d_query_pre, d_key_pre, d_value], axis=2)
        .reshape(tok_count, 3, model_width)
        .astype(jnp.bfloat16)
    )
    d_one = jnp.einsum("tkc,dkc->td", d_qkv, b_qkv, preferred_element_type=jnp.float32)
    d_two = jnp.einsum("tjc,djc->td", d_pre_low, b_up, preferred_element_type=jnp.float32)
    d_inputs, d_vectors = norm_back((d_one, d_two))
    input_grad = upstream + d_inputs
    out_total = jnp.sum(upstream, axis=0)[None]
    bias_rows = jnp.concatenate(
        [
            jnp.zeros((4, model_width), jnp.float32),
            jnp.sum(d_qkv.astype(jnp.float32), axis=0),
            out_total,
            jnp.sum(d_pre_low.astype(jnp.float32), axis=0),
            out_total,
        ],
        axis=0,
    )
    vector_term = d_vectors + bias_rows
    pairs = (
        (h_one[:, None], d_qkv),
        (attn_in[:, None], cotangent[:, None]),
        (h_two[:, None], d_pre_low),
        (act_low, cotangent[:, None]),
    )
    parts = [
        lax.psum_scatter(
            term_of(inputs_of, cot_of, model_width, shard_rows * lax.axis_size("wide")),
            "wide",
            scatter_dimension=0,
            tiled=True,
        )
        for inputs_of, cot_of in pairs
    ]
    summed = jnp.concatenate(parts, axis=1)
    packed = (
        jnp.zeros((shard_rows, lax.axis_size("narrow") * capacity, model_width), jnp.float32)
        .at[:, slot_of]
        .set(summed)
    )
    mine = lax.psum_scatter(packed, "narrow", scatter_dimension=1, tiled=True)
    block_square = jnp.sum(mine * mine)
    vector_total, square_total = lax.psum((vector_term, block_square), ("wide", "narrow"))
    grad_norm = jnp.sqrt(square_total + jnp.sum(vector_total * vector_total))
    clip_factor = jnp.minimum(1.0, 1.0 / (grad_norm + 1e-06))
    step_float = step_count[0].astype(jnp.float32)
    first_fix = 1.0 - jnp.power(beta_first, step_float)
    second_fix = 1.0 - jnp.power(beta_second, step_float)
    owned = (jnp.arange(capacity) < jnp.sum((owners == narrow_index).astype(jnp.int32)))[
        None, :, None
    ]
    block_grads = jnp.where(owned, mine * clip_factor, 0.0)
    new_master, new_first, new_second = adam_update(
        block_grads, master, moment_one, moment_two, learn_rate, weight_decay, first_fix, second_fix
    )
    new_master = jnp.where(owned, new_master, 0.0)
    new_first = jnp.where(owned, new_first, 0.0)
    new_second = jnp.where(owned, new_second, 0.0)
    new_copies = new_master.astype(jnp.bfloat16)
    vector_grads = vector_total * clip_factor
    new_vectors, vector_first, vector_second = adam_update(
        vector_grads, vectors, vector_one, vector_two, vector_rate, 0.0, first_fix, second_fix
    )
    return (
        layer_out,
        input_grad,
        grad_norm,
        block_grads,
        new_master,
        new_first,
        new_second,
        new_copies,
        vector_grads,
        new_vectors,
        vector_first,
        vector_second,
    )


def solution(mesh):
    in_specs = (
        P(("wide", "narrow"), None),
        P(("wide", "narrow"), None),
        P(("wide", "narrow"), None),
        P(),
        P(),
        P("wide", "narrow", None),
        P("wide", "narrow", None),
        P("wide", "narrow", None),
        P(),
        P(),
        P(),
    )
    out_specs = (
        P(("wide", "narrow"), None),
        P(("wide", "narrow"), None),
        P(),
        P("wide", "narrow", None),
        P("wide", "narrow", None),
        P("wide", "narrow", None),
        P("wide", "narrow", None),
        P("wide", "narrow", None),
        P(),
        P(),
        P(),
        P(),
    )
    return jax.shard_map(
        per_device, mesh=mesh, in_specs=in_specs, out_specs=out_specs, check_vma=False
    )
```

profile of v0, /device:TPU:0, one launch (start us, length us, event | category | flops | bytes accessed | tf_op | source)
XLA Modules:
  0.0 905.7 jit_solution(8391424197243354387)
XLA Ops:
  10.5 72.4 %all-gather.6.cloned.1.call-done = bf16[96,24,768]{2,0,1:T(8,128)(2,1)} async-done(((bf16[96,6,768]{2,0,1:T(8,128)(2,1)}), bf16[96,24,768]{2,0,1:T(8,128)(2,1)}) %all-gather.6.cloned.1.call-update) | async-done | bytes 3538960 | tf_op jit(solution)/shard_map/all_gather | solution.py:111
  92.0 17.3 %all-gather.10.cloned.1.call-done = bf16[768,1,768]{2,0,1:T(8,128)(2,1)} async-done(((bf16[96,1,768]{2,0,1:T(8,128)(2,1)}), bf16[768,1,768]{2,0,1:T(8,128)(2,1)}) %all-gather.10.cloned.1.call-update) | async-done | bytes 1179664 | tf_op jit(solution)/shard_map/all_gather | solution.py:115
  117.7 28.2 %all-gather.8.cloned.1.call-done = bf16[768,3,768]{2,0,1:T(8,128)(2,1)} async-done(((bf16[96,3,768]{2,0,1:T(8,128)(2,1)}), bf16[768,3,768]{2,0,1:T(8,128)(2,1)}) %all-gather.8.cloned.1.call-update) | async-done | bytes 3538960 | tf_op jit(solution)/shard_map/all_gather | solution.py:115
  145.8 8.6 broadcast_add_fusion
  154.5 9.8 %copy.89 = f32[1024,3,768]{0,2,1:T(8,128)} copy(f32[1024,3,768]{2,0,1:T(8,128)} %broadcast_add_fusion) | data formatting | bytes 18874368 | tf_op jit(solution)/shard_map/add | solution.py:124
  164.2 13.4 %reshape.204 = f32[2,512,3,12,64]{1,0,4,3,2:T(2,128)} reshape(f32[1024,3,768]{0,2,1:T(8,128)} %copy.89) | data formatting | bytes 18874368 | tf_op jit(solution)/shard_map/reshape | solution.py:125
  188.2 10.7 %fusion.19 = (f32[2,12,512]{2,1,0:T(8,128)S(1)}, f32[2,12,512,512]{2,3,1,0:T(8,128)}) fusion(pred[2,512,512]{1,2,0:T(8,128)(4,1)S(1)} %compare_and_fusion, bf16[2,512,12,48]{1,3,2,0:T(8,128)(2,1)S(1)} %slice.140, bf16[2,512,12,16]{1,3,2,0:T(8,128)(2,1)S(1)} %get-tuple-element.61, bf16[2,512,12,48]{1,3,2,0:T(8,128)(2,1)S(1)} %slice.141, ...), kind=kOutput, calls=%fused_computation.44 | convolution fusion | flops 830459904 | bytes 28884992 | tf_op jit(solution)/shard_map/sqhd,skhd->shqk/dot_general | solution.py:70
  198.9 11.2 %fusion = f32[2,12,512]{2,1,0:T(8,128)S(1)} fusion(f32[2,12,512]{2,1,0:T(8,128)S(1)} %get-tuple-element.68, f32[2,12,512,512]{2,3,1,0:T(8,128)} %get-tuple-element.69, pred[2,512,512]{1,2,0:T(8,128)(4,1)S(1)} %compare_and_fusion), kind=kLoop, calls=%fused_computation.8 | loop fusion | flops 25153536 | bytes 25788416 | tf_op jit(solution)/shard_map/reduce_sum | solution.py:139
  210.1 12.5 %fusion.55 = bf16[2,512,12,64]{1,3,2,0:T(8,128)(2,1)S(1)} fusion(f32[2,12,512]{2,1,0:T(8,128)S(1)} %fusion, f32[2,12,512]{2,1,0:T(8,128)S(1)} %get-tuple-element.68, f32[2,12,512,512]{2,3,1,0:T(8,128)} %get-tuple-element.69, pred[2,512,512]{1,2,0:T(8,128)(4,1)S(1)} %compare_and_fusion, bf16[2,512,1,12,64]{1,0,4,3,2:T(2,128)(2,1)S(1)} %slice.106), kind=kOutput, calls=%fused_computation.112 | convolution fusion | flops 837550080 | bytes 28934144 | tf_op jit(solution)/shard_map/shqk,skhd->sqhd/dot_general | solution.py:142
  228.6 17.2 %multiply_reduce_fusion = (f32[2,12,512]{2,1,0:T(8,128)S(1)}, f32[2,12,512,512]{2,3,1,0:T(8,128)}) fusion(f32[2,12,512]{2,1,0:T(8,128)S(1)} %log_add_fusion, f32[2,12,512,512]{2,3,1,0:T(8,128)} %get-tuple-element.69, pred[2,512,512]{1,2,0:T(8,128)(4,1)S(1)} %compare_and_fusion, bf16[2,512,1,12,64]{1,0,4,3,2:T(2,128)(2,1)} %copy-done.13, ...), kind=kOutput, calls=%fused_computation.3 | convolution fusion | flops 836751360 | bytes 54099968 | tf_op jit(solution)/shard_map/sqhd,skhd->shqk/dot_general | solution.py:181
  245.8 21.7 %multiply_convert_fusion = bf16[2,12,512,512]{2,3,1,0:T(8,128)(2,1)} fusion(f32[2,12,512,512]{2,3,1,0:T(8,128)} %get-tuple-element.72, f32[2,12,512]{2,1,0:T(8,128)S(1)} %get-tuple-element.71, f32[2,12,512]{2,1,0:T(8,128)S(1)} %log_add_fusion, f32[2,12,512,512]{2,3,1,0:T(8,128)} %get-tuple-element.69, pred[2,512,512]{1,2,0:T(8,128)(4,1)S(1)} %compare_and_fusion), kind=kLoop, calls=%fused_computation.2 | loop fusion | flops 37748736 | bytes 63537152 | tf_op jit(solution)/shard_map/convert_element_type | solution.py:182
  267.5 10.2 %multiply_bitcast_fusion = f32[2,512,12,64]{1,3,2,0:T(8,128)} fusion(bf16[2,12,512,512]{2,3,1,0:T(8,128)(2,1)} %multiply_convert_fusion, bf16[2,512,12,48]{1,3,2,0:T(8,128)(2,1)S(1)} %slice.141, bf16[2,512,12,16]{1,3,2,0:T(8,128)(2,1)S(1)} %copy-done.30), kind=kOutput, calls=%fused_computation.84 | convolution fusion | flops 809238528 | bytes 17301504 | tf_op jit(solution)/shard_map/shqk,sqhd->skhd/dot_general | solution.py:188
  308.5 11.8 %fusion.51 = bf16[2,512,12,64]{1,3,2,0:T(8,128)(2,1)S(1)} fusion(f32[2,12,512]{2,1,0:T(8,128)S(1)} %log_add_fusion, f32[2,12,512,512]{2,3,1,0:T(8,128)} %get-tuple-element.69, pred[2,512,512]{1,2,0:T(8,128)(4,1)S(1)} %copy-done.6, bf16[2,512,12,64]{1,0,3,2:T(2,128)(2,1)S(1)} %copy-done.12), kind=kOutput, calls=%fused_computation.110 | convolution fusion | flops 831258624 | bytes 28884992 | tf_op jit(solution)/shard_map/shqk,sqhd->skhd/dot_general | solution.py:175
  327.2 9.1 %fusion.69 = f32[3,768,768]{2,1,0:T(8,128)} fusion(bf16[1024,768]{1,0:T(8,128)(2,1)S(1)} %copy-done.2, f32[768]{0:T(1024)S(1)} %get-tuple-element.22, f32[768]{0:T(1024)S(1)} %get-tuple-element.23, f32[1024]{0:T(1024)S(1)} %fusion.79, f32[1024]{0:T(1024)S(1)} %broadcast_multiply_fusion.2, bf16[1024,1,768]{2,0,1:T(8,128)(2,1)} %copy.106, ...), kind=kOutput, calls=%fused_computation.135 | convolution fusion | flops 3633315840 | bytes 13383680 | tf_op jit(solution)/shard_map/tar,tbc->rabc/dot_general | solution.py:85
  345.0 9.9 %fusion.40 = (u8[1024,768]{1,0:T(8,128)(4,1)S(1)}, u8[1024,768]{1,0:T(8,128)(4,1)S(1)}, f32[1024,4,768]{2,0,1:T(8,128)S(1)}) fusion(f32[4,768]{1,0:T(4,128)S(1)} %copy-done.33, bf16[768,4,768]{2,0,1:T(8,128)(2,1)} %all-gather.12.cloned.1.call-done, bf16[1024,768]{1,0:T(8,128)(2,1)S(1)} %copy-done.2, f32[768]{0:T(1024)S(1)} %copy-done.44, ...), kind=kOutput, calls=%fused_computation.88 | convolution fusion | flops 4879024128 | bytes 20473856 | tf_op jit(solution)/shard_map/td,djc->tjc/dot_general | solution.py:148
  360.7 30.7 %multiply_convert_fusion.1 = (bf16[1024,4,768]{2,0,1:T(8,128)(2,1)}, f32[1024,4,768]{2,0,1:T(8,128)}) fusion(f32[1024,4,768]{2,0,1:T(8,128)S(1)} %get-tuple-element.70, f32[4,768]{1,0:T(4,128)S(1)} %copy-done.33, u8[1024,768]{1,0:T(8,128)(4,1)S(1)} %get-tuple-element.13, u8[1024,768]{1,0:T(8,128)(4,1)S(1)} %get-tuple-element.12), kind=kLoop, calls=%fused_computation.29 | loop fusion | flops 223346688 | bytes 33042432 | tf_op jit(solution)/shard_map/convert_element_type | solution.py:152
  391.4 14.7 %convert_reduce_fusion = (f32[4,768]{1,0:T(4,128)}, bf16[1024,4,768]{2,0,1:T(8,128)(2,1)S(1)}) fusion(f32[1024,4,768]{2,0,1:T(8,128)} %get-tuple-element.41, bf16[768,4,768]{2,0,1:T(8,128)(2,1)} %all-gather.14.cloned.1.call-done, bf16[1024,768]{1,0:T(8,128)(2,1)S(1)} %copy-done.25, f32[1024,4,768]{2,0,1:T(8,128)} %copy-done.4, f32[4,768]{1,0:T(4,128)S(1)} %copy-done.33), kind=kOutput, calls=%fused_computation.27 | convolution fusion | flops 4885312512 | bytes 37773312 | tf_op jit(solution)/shard_map/tc,rjc->tjr/dot_general | solution.py:167
  416.8 12.1 %copy.109 = f32[768,4,768]{2,1,0:T(4,128)} copy(f32[768,4,768]{0,2,1:T(8,128)} %convolution_bitcast_fusion.1) | data formatting | bytes 18874368 | tf_op jit(solution)/shard_map/reshape | solution.py:86
  428.9 10.3 %convolution_bitcast_fusion = f32[768,4,768]{2,0,1:T(8,128)} fusion(bf16[1024,4,768]{2,0,1:T(8,128)(2,1)} %get-tuple-element.40, bf16[1024,768]{1,0:T(8,128)(2,1)S(1)} %copy-done.25), kind=kOutput, calls=%fused_computation.62 | convolution fusion | flops 4831838208 | bytes 17301504 | tf_op jit(solution)/shard_map/tar,tbc->rabc/dot_general | solution.py:85
  439.2 13.4 %copy.111 = f32[768,4,768]{2,1,0:T(4,128)} copy(f32[768,4,768]{2,0,1:T(8,128)} %convolution_bitcast_fusion) | data formatting | bytes 18874368 | tf_op jit(solution)/shard_map/reshape | solution.py:86
  458.1 235.2 %all-reduce.18.cloned.1.call-done = (f32[768,4,768]{2,1,0:T(4,128)}, f32[768,4,768]{2,1,0:T(4,128)}) async-done(((f32[768,4,768]{2,1,0:T(4,128)}, f32[768,4,768]{2,1,0:T(4,128)}), (f32[768,4,768]{2,1,0:T(4,128)}, f32[768,4,768]{2,1,0:T(4,128)})) %all-reduce.18.cloned.1.call-update) | async-done | bytes 18874384
  731.0 101.8 %reduce-scatter.8.cloned.1.call-done = f32[96,6,768]{2,0,1:T(8,128)} async-done(((f32[96,24,768]{2,0,1:T(8,128)}), f32[96,6,768]{2,0,1:T(8,128)}) %reduce-scatter.8.cloned.1.call-update) | async-done | bytes 1769488 | tf_op jit(solution)/shard_map/reduce_scatter | solution.py:234
  835.4 10.0 %fusion.37 = bf16[1024,768]{1,0:T(8,128)(2,1)} fusion(bf16[1024,768]{1,0:T(8,128)(2,1)S(1)} %copy-done.3, f32[1024,768]{1,0:T(8,128)} %fusion.60, bf16[1024,4,768]{2,0,1:T(8,128)(2,1)} %get-tuple-element.40, bf16[768,4,768]{2,0,1:T(8,128)(2,1)} %all-gather.14.cloned.1.call-done, f32[768]{0:T(1024)S(1)} %copy-done.43, f32[768]{0:T(1024)S(1)} %copy-done.42), kind=kOutput, calls=%fused_computation.73 | convolution fusion | flops 4836556800 | bytes 17307648 | tf_op jit(solution)/shard_map/tjr,rjc->tc/dot_general | solution.py:154
  845.4 41.6 %all-reduce.14 = (f32[]{:T(128)}, f32[13,768]{1,0:T(8,128)S(1)}) all-reduce(f32[]{:T(128)} %multiply_reduce_fusion.1, f32[13,768]{1,0:T(8,128)S(1)} %add_add_fusion.1), channel_id=1, replica_groups=mesh['wide'=8,'narrow'=4] {'wide','narrow'}, use_global_device_ids=true, to_apply=%region_18.19 | all-reduce | flops 9985 | bytes 79880 | tf_op jit(solution)/shard_map/psum | solution.py:236
  (225 shorter events, 153.0 us)
Async XLA Ops:
  7.2 75.7 %all-gather.6.cloned.1.call-start = ((), (), s32[]{:S(2)}) async-start(), calls=%async_computation.3 | async-start | bytes 4423680 | tf_op jit(solution)/shard_map/all_gather | solution.py:111
  9.7 99.6 %all-gather.10.cloned.1.call-start = ((), (), s32[]{:S(2)}) async-start(), calls=%async_computation.5 | async-start | bytes 1327104 | tf_op jit(solution)/shard_map/all_gather | solution.py:115
  86.5 59.3 %all-gather.8.cloned.1.call-start = ((), (), s32[]{:S(2)}) async-start(), calls=%async_computation.4 | async-start | bytes 3981312 | tf_op jit(solution)/shard_map/all_gather | solution.py:115
  87.4 257.0 %all-gather.12.cloned.1.call-start = ((), (), s32[]{:S(2)}) async-start(), calls=%async_computation.6 | async-start | bytes 5308416 | tf_op jit(solution)/shard_map/all_gather | solution.py:115
  88.6 302.7 %all-gather.14.cloned.1.call-start = ((), (), s32[]{:S(2)}) async-start(), calls=%async_computation.7 | async-start | bytes 5308416 | tf_op jit(solution)/shard_map/all_gather | solution.py:115
  91.5 22.2 %copy-start.36 = (f32[1024]{0:T(1024)}, f32[1024]{0:T(1024)S(1)}, u32[]{:S(2)}) copy-start(f32[1024]{0:T(1024)S(1)} %fusion.34) | copy-start | bytes 12292
  91.9 153.8 %copy-start.5 = (pred[2,512,512]{1,2,0:T(8,128)(4,1)}, pred[2,512,512]{1,2,0:T(8,128)(4,1)S(1)}, u32[]{:S(2)}) copy-start(pred[2,512,512]{1,2,0:T(8,128)(4,1)S(1)} %compare_and_fusion) | copy-start | bytes 1572868
  92.0 362.5 %reduce-scatter.6.cloned.1.call-start = ((), (), s32[]{:S(2)}) async-start(), calls=%async_computation.8 | async-start | bytes 2654208 | tf_op jit(solution)/shard_map/reduce_scatter | solution.py:220
  187.7 22.4 %copy-start.13 = (bf16[2,512,1,12,64]{1,0,4,3,2:T(2,128)(2,1)}, bf16[2,512,1,12,64]{1,0,4,3,2:T(2,128)(2,1)S(1)}, u32[]{:S(2)}) copy-start(bf16[2,512,1,12,64]{1,0,4,3,2:T(2,128)(2,1)S(1)} %slice.106) | copy-start | bytes 4718596
  188.1 10.7 %copy-start.27 = (bf16[2,512,12,16]{1,3,2,0:T(8,128)(2,1)}, bf16[2,512,12,16]{1,3,2,0:T(8,128)(2,1)S(1)}, u32[]{:S(2)}) copy-start(bf16[2,512,12,16]{1,3,2,0:T(8,128)(2,1)S(1)} %get-tuple-element.61) | copy-start | bytes 1179652
  188.1 10.7 %copy-start.29 = (bf16[2,512,12,16]{1,3,2,0:T(8,128)(2,1)}, bf16[2,512,12,16]{1,3,2,0:T(8,128)(2,1)S(1)}, u32[]{:S(2)}) copy-start(bf16[2,512,12,16]{1,3,2,0:T(8,128)(2,1)S(1)} %get-tuple-element.60) | copy-start | bytes 1179652
  245.8 21.7 %copy-start.30 = (bf16[2,512,12,16]{1,3,2,0:T(8,128)(2,1)S(1)}, bf16[2,512,12,16]{1,3,2,0:T(8,128)(2,1)}, u32[]{:S(2)}) copy-start(bf16[2,512,12,16]{1,3,2,0:T(8,128)(2,1)} %copy-done.29) | copy-start | bytes 1179652
  267.5 10.2 %copy-start.20 = (bf16[2,512,12,48]{1,3,2,0:T(8,128)(2,1)S(1)}, bf16[2,512,12,48]{1,3,2,0:T(8,128)(2,1)}, u32[]{:S(2)}) copy-start(bf16[2,512,12,48]{1,3,2,0:T(8,128)(2,1)} %copy-done.19) | copy-start | bytes 3538948
  267.5 10.2 %copy-start.28 = (bf16[2,512,12,16]{1,3,2,0:T(8,128)(2,1)S(1)}, bf16[2,512,12,16]{1,3,2,0:T(8,128)(2,1)}, u32[]{:S(2)}) copy-start(bf16[2,512,12,16]{1,3,2,0:T(8,128)(2,1)} %copy-done.27) | copy-start | bytes 1179652
  284.4 171.4 %reduce-scatter.10.cloned.1.call-start = ((), (), s32[]{:S(2)}) async-start(), calls=%async_computation.10 | async-start | bytes 7962624
  292.1 6.8 copy-start.21
  344.3 348.9 %all-reduce.18.cloned.1.call-start = ((), (), s32[]{:S(2)}) async-start(), calls=%async_computation.11 | async-start | bytes 37748736
  360.7 30.7 %copy-start.25 = (bf16[1024,768]{1,0:T(8,128)(2,1)S(1)}, bf16[1024,768]{1,0:T(8,128)(2,1)}, u32[]{:S(2)}) copy-start(bf16[1024,768]{1,0:T(8,128)(2,1)} %param.13) | copy-start | bytes 4718596
  452.6 380.2 %reduce-scatter.8.cloned.1.call-start = ((), (), s32[]{:S(2)}) async-start(), calls=%async_computation.9 | async-start | bytes 8847360 | tf_op jit(solution)/shard_map/reduce_scatter | solution.py:234
  713.8 7.1 slice-start.1
  713.8 7.1 slice-start.3
  728.7 106.7 %copy-start.42 = (f32[768]{0:T(1024)S(1)}, f32[768]{0:T(1024)}, u32[]{:S(2)}) copy-start(f32[768]{0:T(1024)} %get-tuple-element.19) | copy-start | bytes 9220
  728.7 106.7 %copy-start.43 = (f32[768]{0:T(1024)S(1)}, f32[768]{0:T(1024)}, u32[]{:S(2)}) copy-start(f32[768]{0:T(1024)} %get-tuple-element.24) | copy-start | bytes 9220
  835.4 53.6 %copy-start.7 = (f32[96,6,768]{2,0,1:T(8,128)S(1)}, f32[96,6,768]{2,0,1:T(8,128)}, u32[]{:S(2)}) copy-start(f32[96,6,768]{2,0,1:T(8,128)} %param.16) | copy-start | bytes 5308420
  (41 other events, 134.7 us)
Sparse Core Ops, SparseCore 0:
  10.2 72.6 all-gather.5
  86.7 22.6 all-gather.9
  111.8 33.9 all-gather.7
  147.6 38.9 all-gather.11
  188.3 38.9 all-gather.13
  284.5 42.6 reduce-scatter.5
  344.5 65.7 reduce-scatter.9
  452.7 240.4 all-reduce.17
  709.2 123.5 reduce-scatter.7
where the time goes:
time: 911 us; the launch traced here: 906 us
  waiting for transfers between devices  455 us (50%)
  matrix products  160 us (18%)
  local copies, waits for them, and re-layouts  137 us (15%)
  other arithmetic  92.9 us (10%)
  blocking collectives  41.6 us (5%)
  between operations  19 us (2%)
    unnamed x11, waiting for transfers between devices  235 us
    reduce_scatter x1, waiting for transfers between devices, per_device(): mine = lax.psum_scatter(packed, 'narrow', scatter_dimension=1, tiled=True)  102 us
    all_gather x1, waiting for transfers between devices, per_device(): lax.all_gather(master.astype(jnp.bfloat16), 'narrow', axis=1, tiled=True)  72.4 us
    all_gather x4, waiting for transfers between devices, forward_weights(): return lax.all_gather(shard, 'wide', axis=0, tiled=True)  45.5 us
    psum x1, blocking collectives, per_device(): lax.psum((vector_term, block_square), ('wide', 'narrow'))  41.6 us
    convert_element_type x1, other arithmetic, per_device(): act_low = act.astype(jnp.bfloat16)  30.7 us
    dot_general x4, matrix products, term_of(): jnp.einsum('tar,tbc->rabc', in_piece, cot_rows, preferred_element_type=jn...  30.2 us
    unnamed x115, local copies, waits for them, and re-layouts  26 us
  transfers between devices with their start and end apart: 9, of which 5 were waited for; matrix products, arithmetic and copies ran while one was open for 37% of the time, Pallas kernels for 0%

commit v1 on v0

v1 whole, which is shorter than its diff:
```python
from functools import partial

import jax
import jax.numpy as jnp
from jax import lax
from jax.experimental import pallas as pl
from jax.experimental.pallas import tpu as pltpu
from jax.sharding import PartitionSpec as P

D = 768
HEADS = 12
HEAD = 64
ROT = 16
FF = 3072
SPREAD = FF // D

norm_epsilon = 1e-05
beta_first = 0.5
beta_second = 0.5
adam_epsilon = 1e-08
learn_rate = 0.02
vector_rate = 0.1
weight_decay = 0.1
masked_fill = -1e30
rope_base = 10000.0
LOG2E = 1.4426950408889634

BF = jnp.bfloat16
F32 = jnp.float32
MB = 1 << 20
ANY = pl.BlockSpec(memory_space=pl.ANY)
SMEM = pl.BlockSpec(memory_space=pltpu.SMEM)


def dot(a, b):
    return lax.dot_general(a, b, (((1,), (0,)), ((), ())), preferred_element_type=F32)


def dot_nt(a, b):
    return lax.dot_general(a, b, (((1,), (1,)), ((), ())), preferred_element_type=F32)


def dot_tn(a, b):
    return lax.dot_general(a, b, (((0,), (0,)), ((), ())), preferred_element_type=F32)


def params(mib, flops=0, moved=0, **more):
    return dict(
        compiler_params=pltpu.CompilerParams(vmem_limit_bytes=int(mib * MB), **more),
        cost_estimate=pl.CostEstimate(
            flops=int(flops), bytes_accessed=int(moved), transcendentals=0
        ),
    )


class Group:
    def __init__(self, arrays, plan):
        self.arrays = tuple(arrays)
        self.plan = plan


def row_of(spec, rows, me):
    if spec[0] == "at":
        return spec[1]
    return pl.multiple_of((me ^ spec[1]) * rows, rows)


def weight_copies(group, refs, i, dst, sems, me):
    copies = []
    for n, (array, lead, rows, spec) in enumerate(group.plan(i)):
        copies.append(
            pltpu.make_async_copy(
                refs[array].at[lead], dst.at[pl.ds(row_of(spec, rows, me), rows)], sems.at[n]
            )
        )
    return copies


def grad_copies(plan, refs, i, src, sems, me):
    copies = []
    for n, (array, lead, rows, spec) in enumerate(plan(i)):
        copies.append(
            pltpu.make_async_copy(
                src.at[pl.ds(row_of(spec, rows, me), rows)], refs[array].at[lead], sems.at[n]
            )
        )
    return copies


def norms_of(x):
    mean = jnp.mean(x, axis=-1, keepdims=True)
    centred = x - mean
    scale = lax.rsqrt(jnp.mean(centred * centred, axis=-1, keepdims=True) + norm_epsilon)
    return centred * scale, scale


def layer_norms(tokens, vectors):
    rows = tokens.shape[0]
    tile = 256

    def body(x_ref, v_ref, one_ref, two_ref):
        xhat, _ = norms_of(x_ref[...].astype(F32))
        one_ref[...] = (xhat * v_ref[0:1] + v_ref[1:2]).astype(BF)
        two_ref[...] = (xhat * v_ref[2:3] + v_ref[3:4]).astype(BF)

    spec = pl.BlockSpec((tile, D), lambda t: (t, 0))
    return pl.pallas_call(
        body,
        grid=(rows // tile,),
        in_specs=[spec, pl.BlockSpec(vectors.shape, lambda t: (0, 0))],
        out_specs=[spec, spec],
        out_shape=[jax.ShapeDtypeStruct((rows, D), BF)] * 2,
        **params(16, 20 * rows * D, 6 * rows * D),
    )(tokens, vectors)


def pack_owned(masters, table, groups):
    rows = masters.shape[1]

    def body(t_ref, m_ref, *outs):
        for out, blocks in zip(outs, groups):
            for i, b in enumerate(blocks):
                value = m_ref[t_ref[0, b]]
                out[i] = jnp.where(t_ref[1, b] > 0, value, 0.0).astype(BF)

    return pl.pallas_call(
        body,
        in_specs=[SMEM, pl.BlockSpec(memory_space=pltpu.VMEM)],
        out_specs=[pl.BlockSpec(memory_space=pltpu.VMEM)] * len(groups),
        out_shape=[jax.ShapeDtypeStruct((len(g), rows, D), BF) for g in groups],
        **params(16, rows * D * 12, rows * D * 4 * 12),
    )(table, masters)


def gelu_pair(z):
    size = jnp.abs(z)
    t = pl.reciprocal(1.0 + (0.3275911 * 0.7071067811865476) * size)
    bell = jnp.exp2((-0.5 * LOG2E) * (z * z))
    poly = 0.5 * 1.061405429
    for c in (-1.453152027, 1.421413741, -0.284496736, 0.254829592):
        poly = poly * t + 0.5 * c
    tail = poly * t * bell
    cdf = jnp.where(z >= 0.0, 1.0 - tail, tail)
    return z * cdf, cdf + z * (bell * 0.3989422804014327)


def mlp_chunk(me, h_two, cot, bias, group, i_up, i_down, outs, plan):
    rows = h_two.shape[0]
    tile = rows // 2
    na, no = len(group.arrays), len(outs)
    n_in, n_out = len(group.plan(0)), len(plan(0))

    def body(me_ref, h_ref, y_ref, b_ref, *rest):
        w_refs = rest[:na]
        act_ref, dz_ref, db_ref = rest[na : na + 3]
        o_refs = rest[na + 3 : na + 3 + no]
        w_up, w_down, acc_up, acc_down, low, in_sem, out_sem = rest[na + 3 + no :]
        step = pl.program_id(0)
        me_id = me_ref[0]

        @pl.when(step == 0)
        def _():
            ups = weight_copies(group, w_refs, i_up, w_up, in_sem.at[0], me_id)
            downs = weight_copies(group, w_refs, i_down, w_down, in_sem.at[1], me_id)
            for c in ups + downs:
                c.start()
            for c in ups + downs:
                c.wait()

        part = 256
        sums = jnp.zeros((1, D), F32)
        for p in range(tile // part):
            at = pl.ds(p * part, part)
            h = h_ref[at]
            y = y_ref[at]
            z = dot(h, w_up[...]) + b_ref[...]
            u = dot_nt(y, w_down[...])
            act, slope = gelu_pair(z)
            dz = (u * slope).astype(BF)
            act_ref[at] = act.astype(BF)
            dz_ref[at] = dz
            sums = sums + jnp.sum(dz.astype(F32), axis=0, keepdims=True)
        d_up = dot_tn(h_ref[...], dz_ref[...])
        d_down = dot_tn(act_ref[...], y_ref[...])

        @pl.when(step == 0)
        def _():
            acc_up[...] = d_up
            acc_down[...] = d_down
            db_ref[...] = sums

        @pl.when(step == 1)
        def _():
            db_ref[...] += sums
            low[0] = (acc_up[...] + d_up).astype(BF)
            low[1] = (acc_down[...] + d_down).astype(BF)
            ups = grad_copies(plan, o_refs, 0, low.at[0], out_sem.at[0], me_id)
            downs = grad_copies(plan, o_refs, 1, low.at[1], out_sem.at[1], me_id)
            for c in ups + downs:
                c.start()
            for c in ups + downs:
                c.wait()

    spec = pl.BlockSpec((tile, D), lambda t: (t, 0))
    row = pl.BlockSpec((1, D), lambda t: (0, 0))
    act, dz, db, *grads = pl.pallas_call(
        body,
        grid=(2,),
        in_specs=[SMEM, spec, spec, row] + [ANY] * na,
        out_specs=[spec, spec, row] + [ANY] * no,
        out_shape=[
            jax.ShapeDtypeStruct((rows, D), BF),
            jax.ShapeDtypeStruct((rows, D), BF),
            jax.ShapeDtypeStruct((1, D), F32),
            *outs,
        ],
        scratch_shapes=[
            pltpu.VMEM((D, D), BF),
            pltpu.VMEM((D, D), BF),
            pltpu.VMEM((D, D), F32),
            pltpu.VMEM((D, D), F32),
            pltpu.VMEM((2, D, D), BF),
            pltpu.SemaphoreType.DMA((2, n_in)),
            pltpu.SemaphoreType.DMA((2, n_out)),
        ],
        **params(40, 8 * rows * D * D, 16 * rows * D),
    )(me, h_two, cot, bias, *group.arrays)
    return act, dz, db, grads


def turned(x, cosine, from_right, from_left):
    return (
        x * cosine
        + pltpu.roll(x, 128 - ROT // 2, 1) * from_right
        + pltpu.roll(x, ROT // 2, 1) * from_left
    )


def project(me, h_one, cot, bias, tables, group):
    rows = h_one.shape[0]
    tile = 256
    na, n_in = len(group.arrays), len(group.plan(0))

    def body(me_ref, h_ref, y_ref, b_ref, c_ref, s_ref, *rest):
        w_refs = rest[:na]
        outs = rest[na : na + 4]
        w_all, sems = rest[na + 4 :]
        step = pl.program_id(0)

        def copies(i):
            return weight_copies(group, w_refs, i, w_all.at[i], sems.at[i], me_ref[0])

        @pl.when(step == 0)
        def _():
            for i in range(4):
                for c in copies(i):
                    c.start()

        for i in range(4):

            @pl.when(step == 0)
            def _(i=i):
                for c in copies(i):
                    c.wait()

            if i == 3:
                outs[3][...] = dot_nt(y_ref[...], w_all[3]).astype(BF)
                continue
            value = dot(h_ref[...], w_all[i]) + b_ref[i : i + 1]
            if i == 2:
                outs[2][...] = value.astype(BF)
                continue
            cosine, right, left = c_ref[...], s_ref[0], s_ref[1]
            for j in range(D // 128):
                outs[i][:, j * 128 : (j + 1) * 128] = turned(
                    value[:, j * 128 : (j + 1) * 128], cosine, -right, left
                ).astype(BF)

    spec = pl.BlockSpec((tile, D), lambda t: (t, 0))
    return pl.pallas_call(
        body,
        grid=(rows // tile,),
        in_specs=[
            SMEM,
            spec,
            spec,
            pl.BlockSpec((3, D), lambda t: (0, 0)),
            pl.BlockSpec((tile, 128), lambda t: (t, 0)),
            pl.BlockSpec((2, tile, 128), lambda t: (0, t, 0)),
        ]
        + [ANY] * na,
        out_specs=[spec] * 4,
        out_shape=[jax.ShapeDtypeStruct((rows, D), BF)] * 4,
        scratch_shapes=[pltpu.VMEM((4, D, D), BF), pltpu.SemaphoreType.DMA((4, n_in))],
        **params(32, 8 * rows * D * D, 20 * rows * D),
    )(me, h_one, cot, bias, *tables, *group.arrays)


def attention(q, k, v, da, starts, tables, half_tables, length):
    rows = q.shape[0]
    seqs = rows // length
    half = length // 2
    pair = 128

    def body(q_ref, k_ref, v_ref, d_ref, st_ref, c_ref, s_ref, hc_ref, hs_ref, a_ref, dq_ref, dk_ref, dv_ref, db_ref, mask):
        @pl.when(pl.program_id(1) == 0)
        def _():
            key = lax.broadcasted_iota(jnp.int32, (length, length), 0)
            query = lax.broadcasted_iota(jnp.int32, (length, length), 1)
            seen = (key <= query) & (key >= st_ref[0])
            mask[...] = jnp.where(seen, 0.0, masked_fill)

        q_all, k_all, v_all, d_all = q_ref[...], k_ref[...], v_ref[...], d_ref[...]
        vt, kt = v_all.T, k_all.T
        dt = d_all.T.astype(F32)
        lane = lax.broadcasted_iota(jnp.int32, (length, pair), 1)
        zero = jnp.zeros((), BF)
        at, dqt = [], []
        dv = [jnp.zeros((half, pair), F32)] * 2
        dk = [jnp.zeros((half, pair), F32)] * 2
        for h in range(2):
            mine = (lane >= h * HEAD) & (lane < (h + 1) * HEAD)
            qm = jnp.where(mine, q_all, zero)
            dm = jnp.where(mine, d_all, zero)
            vh, kh = vt[h * HEAD : (h + 1) * HEAD], kt[h * HEAD : (h + 1) * HEAD]
            dh = dt[h * HEAD : (h + 1) * HEAD]
            a_parts, q_parts = [], []
            for b in range(2):
                n = half * (b + 1)
                at_q = slice(b * half, (b + 1) * half)
                s = dot_nt(k_all[:n], qm[at_q]) * (HEAD**-0.5 * LOG2E) + mask[:n, at_q]
                e = jnp.exp2(s - jnp.max(s, axis=0, keepdims=True))
                p = e * (1.0 / jnp.sum(e, axis=0, keepdims=True))
                low = p.astype(BF)
                a_t = dot(vh[:, :n], low)
                total = jnp.sum(dh[:, at_q] * a_t, axis=0, keepdims=True)
                ds = (p * (dot_nt(v_all[:n], dm[at_q]) - total)).astype(BF)
                a_parts.append(a_t)
                q_parts.append(dot(kh[:, :n], ds))
                more_v, more_k = dot(low, dm[at_q]), dot(ds, qm[at_q])
                for c in range(b + 1):
                    dv[c] = dv[c] + more_v[c * half : (c + 1) * half]
                    dk[c] = dk[c] + more_k[c * half : (c + 1) * half]
            at.append(jnp.concatenate(a_parts, axis=1))
            dq = jnp.concatenate(q_parts, axis=1) * HEAD**-0.5
            u, w, cos, sin = dq[0:8], dq[8:16], hc_ref[0], hs_ref[0]
            dqt.append(jnp.concatenate([u * cos + w * sin, w * cos - u * sin, dq[16:]], axis=0))
        a_ref[...] = jnp.concatenate(at, axis=0).astype(BF).T
        dq = jnp.concatenate(dqt, axis=0).astype(BF).T
        dq_ref[...] = dq
        sums = [jnp.sum(dq.astype(F32), axis=0, keepdims=True)]
        sum_k = sum_v = jnp.zeros((1, pair), F32)
        for c in range(2):
            at_k = slice(c * half, (c + 1) * half)
            back = turned(dk[c] * HEAD**-0.5, c_ref[at_k], s_ref[0, at_k], -s_ref[1, at_k]).astype(BF)
            dk_ref[at_k] = back
            sum_k = sum_k + jnp.sum(back.astype(F32), axis=0, keepdims=True)
            value = dv[c].astype(BF)
            dv_ref[at_k] = value
            sum_v = sum_v + jnp.sum(value.astype(F32), axis=0, keepdims=True)
        db_ref[0] = jnp.concatenate(sums + [sum_k, sum_v], axis=0)

    spec = pl.BlockSpec((length, pair), lambda s, h: (s, h))
    a, dq, dk, dv, db = pl.pallas_call(
        body,
        grid=(seqs, D // pair),
        in_specs=[
            spec,
            spec,
            spec,
            spec,
            pl.BlockSpec((1, 1, length), lambda s, h: (s, 0, 0)),
            pl.BlockSpec((length, 128), lambda s, h: (s, 0)),
            pl.BlockSpec((2, length, 128), lambda s, h: (0, s, 0)),
            pl.BlockSpec((1, ROT // 2, length), lambda s, h: (s, 0, 0)),
            pl.BlockSpec((1, ROT // 2, length), lambda s, h: (s, 0, 0)),
        ],
        out_specs=[spec, spec, spec, spec, pl.BlockSpec((1, 3, pair), lambda s, h: (s, 0, h))],
        out_shape=[jax.ShapeDtypeStruct((rows, D), BF)] * 4
        + [jax.ShapeDtypeStruct((seqs, 3, D), F32)],
        scratch_shapes=[pltpu.VMEM((length, length), F32)],
        **params(32, 20e9, 20 * rows * D),
    )(q, k, v, da, starts, *tables, *half_tables)
    return a, dq, dk, dv, jnp.sum(db, axis=0)


def attention_grads(me, h_one, a, cot, dqkv, outs, plan):
    rows = h_one.shape[0]
    no, n_out = len(outs), len(plan(0))

    def body(me_ref, h_ref, a_ref, y_ref, dq_ref, dk_ref, dv_ref, *rest):
        o_refs = rest[:no]
        low, sems = rest[no:]
        pending = []
        for i, (left, right) in enumerate(
            ((h_ref, dq_ref), (h_ref, dk_ref), (h_ref, dv_ref), (a_ref, y_ref))
        ):
            low[i] = dot_tn(left[...], right[...]).astype(BF)
            copies = grad_copies(plan, o_refs, i, low.at[i], sems.at[i], me_ref[0])
            for c in copies:
                c.start()
            pending += copies
        for c in pending:
            c.wait()

    whole = pl.BlockSpec(memory_space=pltpu.VMEM)
    return pl.pallas_call(
        body,
        in_specs=[SMEM] + [whole] * 6,
        out_specs=[ANY] * no,
        out_shape=list(outs),
        scratch_shapes=[pltpu.VMEM((4, D, D), BF), pltpu.SemaphoreType.DMA((4, n_out))],
        **params(40, 8 * rows * D * D, 12 * rows * D),
    )(me, h_one, a, cot, *dqkv)


def finish(me, tokens, cot, vectors, a, dqkv, acts, dzs, blocks):
    rows = tokens.shape[0]
    tile = 256
    groups = []
    for group, _ in blocks:
        if not any(group is g for g in groups):
            groups.append(group)
    first = {}
    flat = []
    for group in groups:
        first[id(group)] = len(flat)
        flat += list(group.arrays)
    n_in = max(len(g.plan(0)) for g in groups)
    nw = len(flat)
    count = len(blocks)
    order = (3, 8, 9, 10, 11, 0, 1, 2, 4, 5, 6, 7)

    def body(me_ref, x_ref, y_ref, v_ref, a_ref, dq_ref, dk_ref, dv_ref, *rest):
        act_refs, dz_refs = rest[:SPREAD], rest[SPREAD : 2 * SPREAD]
        w_refs = rest[2 * SPREAD : 2 * SPREAD + nw]
        out_ref, grad_ref, sum_ref = rest[2 * SPREAD + nw : 2 * SPREAD + nw + 3]
        w_all, sems = rest[2 * SPREAD + nw + 3 :]
        step = pl.program_id(0)

        def copies(b):
            group, i = blocks[b]
            refs = w_refs[first[id(group)] :]
            return weight_copies(group, refs, i, w_all.at[b], sems.at[b], me_ref[0])

        @pl.when(step == 0)
        def _():
            for b in order:
                for c in copies(b):
                    c.start()

        def weight(b):
            @pl.when(step == 0)
            def _():
                for c in copies(b):
                    c.wait()

            return w_all[b]

        x = x_ref[...].astype(F32)
        y = y_ref[...].astype(F32)
        out = dot(a_ref[...], weight(3))
        for j in range(SPREAD):
            out = out + dot(act_refs[j][...], weight(8 + j))
        out_ref[...] = (x + out + (v_ref[7:8] + v_ref[8 + SPREAD : 9 + SPREAD])).astype(BF)
        d_one = dot_nt(dq_ref[...], weight(0))
        d_one = d_one + dot_nt(dk_ref[...], weight(1))
        d_one = d_one + dot_nt(dv_ref[...], weight(2))
        d_two = dot_nt(dz_refs[0][...], weight(4))
        for j in range(1, SPREAD):
            d_two = d_two + dot_nt(dz_refs[j][...], weight(4 + j))
        xhat, scale = norms_of(x)
        e = d_one * v_ref[0:1] + d_two * v_ref[2:3]
        inner = jnp.mean(e * xhat, axis=-1, keepdims=True)
        grad_ref[...] = y + (e - jnp.mean(e, axis=-1, keepdims=True) - xhat * inner) * scale
        sums = jnp.concatenate(
            [
                jnp.sum(term, axis=0, keepdims=True)
                for term in (d_one * xhat, d_one, d_two * xhat, d_two, y)
            ],
            axis=0,
        )

        @pl.when(step == 0)
        def _():
            sum_ref[...] = sums

        @pl.when(step > 0)
        def _():
            sum_ref[...] += sums

    spec = pl.BlockSpec((tile, D), lambda t: (t, 0))
    return pl.pallas_call(
        body,
        grid=(rows // tile,),
        in_specs=[SMEM, spec, spec, pl.BlockSpec(vectors.shape, lambda t: (0, 0))]
        + [spec] * (4 + 2 * SPREAD)
        + [ANY] * nw,
        out_specs=[spec, spec, pl.BlockSpec((5, D), lambda t: (0, 0))],
        out_shape=[
            jax.ShapeDtypeStruct((rows, D), BF),
            jax.ShapeDtypeStruct((rows, D), F32),
            jax.ShapeDtypeStruct((5, D), F32),
        ],
        scratch_shapes=[pltpu.VMEM((count, D, D), BF), pltpu.SemaphoreType.DMA((count, n_in))],
        **params(48, 24 * rows * D * D, 40 * rows * D),
    )(me, tokens, cot, vectors, a, *dqkv, *acts, *dzs, *flat)


def adam_update(gradient, weight, moment, square, rate, decay, first_fix, second_fix):
    moment_new = beta_first * moment + (1.0 - beta_first) * gradient
    square_new = beta_second * square + (1.0 - beta_second) * gradient * gradient
    update = moment_new / first_fix / (jnp.sqrt(square_new / second_fix) + adam_epsilon)
    return (weight - rate * (update + decay * weight), moment_new, square_new)


def update_blocks(block_at, owned, scalars, summed, masters, firsts, seconds):
    slots, rows, _ = masters.shape

    def body(at_ref, own_ref, s_ref, g_ref, w_ref, m_ref, v_ref, g_out, w_out, m_out, v_out, c_out):
        slot = pl.program_id(0)
        keep = own_ref[slot] > 0
        clip, one_fix, two_fix = s_ref[0], s_ref[1], s_ref[2]
        gradient = g_ref[0].astype(F32) * clip
        moment = beta_first * m_ref[0] + (1.0 - beta_first) * gradient
        square = beta_second * v_ref[0] + (1.0 - beta_second) * gradient * gradient
        weight = w_ref[0]
        update = (moment * one_fix) / (jnp.sqrt(square * two_fix) + adam_epsilon)
        new = weight - learn_rate * (update + weight_decay * weight)
        new = jnp.where(keep, new, 0.0)
        g_out[0] = jnp.where(keep, gradient, 0.0)
        w_out[0] = new
        m_out[0] = jnp.where(keep, moment, 0.0)
        v_out[0] = jnp.where(keep, square, 0.0)
        c_out[0] = new.astype(BF)

    own = pl.BlockSpec((1, rows, D), lambda s, at, keep, sc: (s, 0, 0))
    return pl.pallas_call(
        body,
        grid_spec=pltpu.PrefetchScalarGridSpec(
            num_scalar_prefetch=3,
            grid=(slots,),
            in_specs=[pl.BlockSpec((1, rows, D), lambda s, at, keep, sc: (at[s], 0, 0)), own, own, own],
            out_specs=[own] * 5,
        ),
        out_shape=[jax.ShapeDtypeStruct((slots, rows, D), F32)] * 4
        + [jax.ShapeDtypeStruct((slots, rows, D), BF)],
        **params(24, 20 * slots * rows * D, 32 * slots * rows * D),
    )(block_at, owned, scalars, summed, masters, firsts, seconds)


def swap(value, axis, bit):
    size = lax.axis_size(axis)
    return lax.ppermute(value, axis, [(i, i ^ bit) for i in range(size)])


def add(a, b):
    return (a.astype(F32) + b.astype(F32)).astype(BF)


def line_total(value):
    size = lax.axis_size("narrow")
    if size != 4:
        return lax.psum(value.astype(F32), "narrow").astype(BF)
    here = lax.axis_index("narrow")
    value = add(value, lax.ppermute(value, "narrow", [(0, 1), (3, 2)]))
    value = add(value, lax.ppermute(value, "narrow", [(1, 2), (2, 1)]))
    outer = lax.ppermute(value, "narrow", [(1, 0), (2, 3)])
    return jnp.where((here == 0) | (here == 3), outer, value)


CORE, SIDE, UP = 1, 2, 4
CHIPS = (0, SIDE, UP, SIDE | UP)


def gather_wide(value):
    size = lax.axis_size("wide")
    count, rows, _ = value.shape
    full = lax.all_gather(value, "wide", axis=0, tiled=False)
    if rows % 16:
        full = jnp.swapaxes(full, 0, 1).reshape(1, count, D, D)
        size, rows = 1, D
    return Group((full,), lambda i: [(0, (p, i), rows, ("at", rows * p)) for p in range(size)])


def gather_wide_steps(value):
    size = lax.axis_size("wide")
    count, rows, _ = value.shape
    if size != 8 or count % 2:
        return gather_wide(value)
    side, up = swap(value, "wide", SIDE), swap(value, "wide", UP)
    part = count // 2
    diag_a = swap(side[:part], "wide", UP)
    diag_b = swap(up[part:], "wide", SIDE)
    mine = jnp.stack([value, side, up, jnp.concatenate([diag_a, diag_b], axis=0)])
    other = swap(mine, "wide", CORE)
    masks = [(m, 0) for m in CHIPS] + [(m ^ CORE, 1) for m in CHIPS]
    return Group(
        (mine, other),
        lambda i: [(a, (n % 4, i), rows, ("xor", m)) for n, (m, a) in enumerate(masks)],
    )


def grad_layout(count, rows, size):
    if size != 8:
        return [jax.ShapeDtypeStruct((count, D, D), BF)], lambda i: [(0, (i,), D, ("at", 0))]
    part = count // 2
    shape = jax.ShapeDtypeStruct((4, part, rows, D), BF)

    def plan(i):
        which = 0 if i < part else 1
        order = (0, UP, SIDE, SIDE | UP) if which == 0 else CHIPS
        at = i % part
        keep = [(which, (n, at), rows, ("xor", m)) for n, m in enumerate(order)]
        give = [(2 + which, (n, at), rows, ("xor", m ^ CORE)) for n, m in enumerate(order)]
        return keep + give

    return [shape] * 4, plan


def scatter_wide(grads):
    if len(grads) == 1:
        return lax.psum_scatter(grads[0], "wide", scatter_dimension=1, tiled=True)
    keep_a, keep_b, give_a, give_b = grads
    sum_a = add(keep_a, swap(give_a, "wide", CORE))
    sum_b = add(keep_b, swap(give_b, "wide", CORE))
    sum_a = add(sum_a[:2], swap(sum_a[2:], "wide", SIDE))
    sum_b = add(sum_b[:2], swap(sum_b[2:], "wide", UP))
    sum_a = add(sum_a[0], swap(sum_a[1], "wide", UP))
    sum_b = add(sum_b[0], swap(sum_b[1], "wide", SIDE))
    return jnp.concatenate([sum_a, sum_b], axis=0)


def total_all(value):
    for axis in ("wide", "narrow"):
        value = total_axis(value, axis)
    return value


def total_axis(value, axis):
    size = lax.axis_size(axis)
    bit = 1
    while bit < size:
        value = value + swap(value, axis, bit)
        bit *= 2
    return value


def slot_table(owners, capacity):
    number = owners.shape[0]
    order = jnp.arange(number, dtype=jnp.int32)
    before = (owners[:, None] == owners[None, :]) & (order[None, :] < order[:, None])
    return owners * capacity + jnp.sum(before.astype(jnp.int32), axis=1)


def rotary_tables(offsets):
    half = ROT // 2
    freqs = jnp.power(rope_base, -2.0 * jnp.arange(half, dtype=F32) / ROT)
    angle = offsets.astype(F32)[:, None, :] * freqs[None, :, None]
    cosine, sine = jnp.cos(angle), jnp.sin(angle)
    cos_t = jnp.swapaxes(cosine, 1, 2).reshape(-1, half)
    sin_t = jnp.swapaxes(sine, 1, 2).reshape(-1, half)
    rows = cos_t.shape[0]
    none = jnp.zeros((rows, half), F32)
    rest = jnp.zeros((rows, HEAD - ROT), F32)
    lanes = jnp.concatenate([cos_t, cos_t, rest + 1.0] * 2, axis=1)
    right = jnp.concatenate([sin_t, none, rest] * 2, axis=1)
    left = jnp.concatenate([none, sin_t, rest] * 2, axis=1)
    return (lanes, jnp.stack([right, left])), (cosine, sine)


FIRST = (4, 8)
SECOND = (0, 1, 2, 3)
THIRD = (5, 9, 6, 10, 7, 11)


def per_device(tokens, doc_lengths, cotangent, owners, step_count, master, moment_one, moment_two, vectors, vector_one, vector_two):
    rows, capacity, _ = master.shape
    seqs = doc_lengths.shape[0]
    length = tokens.shape[0] // seqs
    blocks = owners.shape[0]
    wide = lax.axis_size("wide")
    narrow_index = lax.axis_index("narrow")
    me = lax.axis_index("wide").astype(jnp.int32).reshape(1)
    masters, firsts, seconds = [jnp.swapaxes(m, 0, 1) for m in (master, moment_one, moment_two)]

    local = slot_table(owners, capacity) - owners * capacity
    is_mine = (owners == narrow_index).astype(jnp.int32)
    order = (FIRST, SECOND, THIRD)
    packed = pack_owned(masters, jnp.stack([local, is_mine]), order)
    shards = [line_total(p) for p in packed]
    g_first = gather_wide_steps(shards[0])
    g_second = gather_wide_steps(shards[1])
    g_third = gather_wide(shards[2])
    place = {}
    for group, ids in ((g_first, FIRST), (g_second, SECOND), (g_third, THIRD)):
        for i, b in enumerate(ids):
            place[b] = (group, i)

    h_one, h_two = layer_norms(tokens, vectors)
    ends = jnp.cumsum(doc_lengths, axis=1)
    position = jnp.arange(length, dtype=jnp.int32)
    passed = position[None, None, :] >= ends[:, :, None]
    start = jnp.sum(jnp.where(passed, doc_lengths[:, :, None], 0), axis=1)
    tables, half_tables = rotary_tables(position[None] - start)

    acts, dzs, dbs, sums = [], [], [], {}
    pair_outs, pair_plan = grad_layout(2, rows, wide)
    four_outs, four_plan = grad_layout(4, rows, wide)

    def chunk(j):
        group, i_up = place[4 + j]
        _, i_down = place[8 + j]
        act, dz, db, grads = mlp_chunk(
            me, h_two, cotangent, vectors[8 + j : 9 + j], group, i_up, i_down, pair_outs, pair_plan
        )
        acts.append(act)
        dzs.append(dz)
        dbs.append(db)
        return scatter_wide(grads)

    scattered = [((4, 8), chunk(0))]
    q, k, v, da = project(me, h_one, cotangent, vectors[4:7], tables, g_second)
    a, *dqkv, db_qkv = attention(q, k, v, da, start[:, None, :], tables, half_tables, length)
    scattered.append((SECOND, scatter_wide(attention_grads(me, h_one, a, cotangent, dqkv, four_outs, four_plan))))
    for j in range(1, SPREAD):
        scattered.append(((4 + j, 8 + j), chunk(j)))
    totals = {}
    square = jnp.zeros((), F32)
    for ids, value in scattered:
        value = line_total(value)
        square = square + jnp.sum(jnp.square(value.astype(F32)))
        for i, b in enumerate(ids):
            totals[b] = value[i]
    summed = jnp.stack([totals[b] for b in range(blocks)])

    layer_out, input_grad, sums = finish(
        me, tokens, cotangent, vectors, a, dqkv, acts, dzs, [place[b] for b in range(blocks)]
    )
    vector_term = jnp.concatenate([sums[0:4], db_qkv, sums[4:5], *dbs, sums[4:5]], axis=0)
    vector_total = total_all(vector_term)
    square_total = total_axis(jnp.broadcast_to(square, (8, 128)), "wide")[0, 0]
    grad_norm = jnp.sqrt(square_total + jnp.sum(vector_total * vector_total))
    clip = jnp.minimum(1.0, 1.0 / (grad_norm + 1e-06))
    step_float = step_count[0].astype(F32)
    first_fix = 1.0 - jnp.power(beta_first, step_float)
    second_fix = 1.0 - jnp.power(beta_second, step_float)

    slot = jnp.arange(capacity, dtype=jnp.int32)
    hit = (owners == narrow_index)[None, :] & (local[None, :] == slot[:, None])
    block_at = jnp.sum(jnp.where(hit, jnp.arange(blocks, dtype=jnp.int32)[None], 0), axis=1)
    owned = jnp.sum(hit.astype(jnp.int32), axis=1)
    scalars = jnp.stack([clip, 1.0 / first_fix, 1.0 / second_fix])
    new = update_blocks(block_at, owned, scalars, summed, masters, firsts, seconds)
    block_grads, new_master, new_first, new_second, new_copies = [jnp.swapaxes(m, 0, 1) for m in new]
    vector_grads = vector_total * clip
    new_vectors, vector_first, vector_second = adam_update(
        vector_grads, vectors, vector_one, vector_two, vector_rate, 0.0, first_fix, second_fix
    )
    return (
        layer_out,
        input_grad,
        grad_norm,
        block_grads,
        new_master,
        new_first,
        new_second,
        new_copies,
        vector_grads,
        new_vectors,
        vector_first,
        vector_second,
    )


def solution(mesh):
    tok = P(("wide", "narrow"), None)
    own = P("wide", "narrow", None)
    return jax.shard_map(
        per_device,
        mesh=mesh,
        in_specs=(tok, tok, tok, P(), P(), own, own, own, P(), P(), P()),
        out_specs=(tok, tok, P(), own, own, own, own, own, P(), P(), P(), P()),
        check_vma=False,
    )
```

time: 911 us -> 559 us (0.61)
  waiting for transfers between devices: 455 us -> 163 us
  Pallas kernels: 0 us -> 174 us
  matrix products: 160 us -> 0 us
  starting transfers between devices: 0.37 us -> 115 us
  local copies, waits for them, and re-layouts: 137 us -> 41.5 us
  other arithmetic: 92.9 us -> 38.4 us
  blocking collectives: 41.6 us -> 0 us
    unnamed x11 -> x1, waiting for transfers between devices: 235 us -> 0.02 us
    pallas_call x0 -> x11, Pallas kernels: none -> 174 us  [the longest x4 54 us: mlp_chunk(): pl.pallas_call(body, grid=(2,), in_specs=[SMEM, spec, spec, row] + [ANY]...]
    ppermute x0 -> x72, waiting for transfers between devices: none -> 163 us  [the longest x48 81.7 us: swap(): return lax.ppermute(value, axis, [(i, i ^ bit) for i in range(size)])]
    dot_general x18 -> x0, matrix products: 160 us -> none  [the longest x4 30.2 us: term_of(): jnp.einsum('tar,tbc->rabc', in_piece, cot_rows, preferred_element_type=jn...]
    all_gather x5 -> x1, waiting for transfers between devices: 118 us -> 0.02 us  [gather_wide(): full = lax.all_gather(value, 'wide', axis=0, tiled=False)]
    ppermute x0 -> x72, starting transfers between devices: none -> 114 us  [the longest x48 56.8 us: swap(): return lax.ppermute(value, axis, [(i, i ^ bit) for i in range(size)])]
    reduce_scatter x2 -> x0, waiting for transfers between devices: 102 us -> none  [the longest x1 102 us: per_device(): mine = lax.psum_scatter(packed, 'narrow', scatter_dimension=1, tiled=True)]
    convert_element_type x5 -> x48, other arithmetic: 60.6 us -> 9.43 us  [the longest x46 9.42 us: add(): return (a.astype(F32) + b.astype(F32)).astype(BF)]
  transfers between devices with their start and end apart: 9 -> 73, of which waited for: 5 -> 36; matrix products, arithmetic and copies ran while one was open for 37% -> 9% of each run, Pallas kernels for 0% -> 30%
where the time goes in v1:
time: 559 us; the launch traced here: 554 us
  Pallas kernels  174 us (31%)
  waiting for transfers between devices  163 us (29%)
  starting transfers between devices  115 us (21%)
  local copies, waits for them, and re-layouts  41.5 us (7%)
  other arithmetic  38.4 us (7%)
  between operations  22.4 us (4%)
    ppermute x48, waiting for transfers between devices, swap(): return lax.ppermute(value, axis, [(i, i ^ bit) for i in range(size)])  81.7 us
    ppermute x48, starting transfers between devices, swap(): return lax.ppermute(value, axis, [(i, i ^ bit) for i in range(size)])  56.8 us
    ppermute x8, waiting for transfers between devices, line_total(): value = add(value, lax.ppermute(value, 'narrow', [(0, 1), (3, 2)]))  55.4 us
    pallas_call x4, Pallas kernels, mlp_chunk(): pl.pallas_call(body, grid=(2,), in_specs=[SMEM, spec, spec, row] + [ANY]...  54 us
    pallas_call x1, Pallas kernels, attention(): pl.pallas_call(body, grid=(seqs, D // pair), in_specs=[spec, spec, spec,...  43.8 us
    ppermute x8, starting transfers between devices, line_total(): value = add(value, lax.ppermute(value, 'narrow', [(0, 1), (3, 2)]))  41.4 us
    pallas_call x1, Pallas kernels, finish(): pl.pallas_call(body, grid=(rows // tile,), in_specs=[SMEM, spec, spec, pl...  40.8 us
    unnamed x130, local copies, waits for them, and re-layouts  26.3 us
  transfers between devices with their start and end apart: 73, of which 36 were waited for; matrix products, arithmetic and copies ran while one was open for 9% of the time, Pallas kernels for 30%

profile of v1, /device:TPU:0, one launch (start us, length us, event | category | flops | bytes accessed | tf_op | source)
XLA Modules:
  0.0 554.4 jit_solution(11178908536975111351)
XLA Ops:
  11.8 5.0 collective-permute-start.16
  18.1 18.6 %collective-permute-done.16 = bf16[6,96,768]{2,1,0:T(8,128)(2,1)S(1)} collective-permute-done((bf16[6,96,768]{2,1,0:T(8,128)(2,1)S(1)}, bf16[6,96,768]{2,1,0:T(8,128)(2,1)S(1)}, u32[]{:S(2)}, u32[]{:S(2)}) %collective-permute-start.16) | collective-permute-done | bytes 884768 | tf_op jit(solution)/shard_map/ppermute | solution.py:566
  37.7 10.5 %collective-permute-done = bf16[4,96,768]{2,1,0:T(8,128)(2,1)S(1)} collective-permute-done((bf16[4,96,768]{2,1,0:T(8,128)(2,1)S(1)}, bf16[4,96,768]{2,1,0:T(8,128)(2,1)S(1)}, u32[]{:S(2)}, u32[]{:S(2)}) %collective-permute-start) | collective-permute-done | bytes 589856 | tf_op jit(solution)/shard_map/ppermute | solution.py:566
  52.1 24.7 %collective-permute-start.8 = (bf16[2,96,768]{2,1,0:T(8,128)(2,1)S(1)}, bf16[2,96,768]{2,1,0:T(8,128)(2,1)S(1)}, u32[]{:S(2)}, u32[]{:S(2)}) collective-permute-start(bf16[2,96,768]{2,1,0:T(8,128)(2,1)S(1)} %get-tuple-element.77), channel_id=1, source_target_pairs={{0,1},{3,2},{4,5},{7,6},{8,9},{11,10},{12,13},{15,14},{16,17},{19,... | collective-permute-start | bytes 884744 | tf_op jit(solution)/shard_map/ppermute | solution.py:566
  81.8 9.8 %collective-permute-done.2 = bf16[4,96,768]{2,1,0:T(8,128)(2,1)S(1)} collective-permute-done((bf16[4,96,768]{2,1,0:T(8,128)(2,1)S(1)}, bf16[4,96,768]{2,1,0:T(8,128)(2,1)S(1)}, u32[]{:S(2)}, u32[]{:S(2)}) %collective-permute-start.2) | collective-permute-done | bytes 589856 | tf_op jit(solution)/shard_map/ppermute | solution.py:568
  98.8 5.8 %collective-permute-done.4 = bf16[4,96,768]{2,1,0:T(8,128)(2,1)S(1)} collective-permute-done((bf16[4,96,768]{2,1,0:T(8,128)(2,1)S(1)}, bf16[4,96,768]{2,1,0:T(8,128)(2,1)S(1)}, u32[]{:S(2)}, u32[]{:S(2)}) %collective-permute-start.4) | collective-permute-done | bytes 589856 | tf_op jit(solution)/shard_map/ppermute | solution.py:554
  106.8 6.0 %collective-permute-done.3 = bf16[4,96,768]{2,1,0:T(8,128)(2,1)S(1)} collective-permute-done((bf16[4,96,768]{2,1,0:T(8,128)(2,1)S(1)}, bf16[4,96,768]{2,1,0:T(8,128)(2,1)S(1)}, u32[]{:S(2)}, u32[]{:S(2)}) %collective-permute-start.3) | collective-permute-done | bytes 589856 | tf_op jit(solution)/shard_map/ppermute | solution.py:554
  117.5 4.6 collective-permute-done.6
  159.6 14.4 %shard_map.206 = (bf16[1024,768]{1,0:T(8,128)(2,1)S(1)}, bf16[1024,768]{1,0:T(8,128)(2,1)S(1)}, f32[1,768]{1,0:T(1,128)S(1)}, bf16[4,1,96,768]{3,2,1,0:T(8,128)(...) custom-call(s32[1]{0:T(128)} %bitcast.me_ref, ...), custom_call_target="tpu_custom_call" | custom-call | flops 4831838208 | bytes 12582912 | tf_op jit(solution)/shard_map/pallas_call | solution.py:206
  174.6 14.6 %shard_map.204 = (bf16[1024,768]{1,0:T(8,128)(2,1)S(1)}, bf16[1024,768]{1,0:T(8,128)(2,1)S(1)}, bf16[1024,768]{1,0:T(8,128)(2,1)S(1)}, bf16[1024,768]{1,0:T(8,128)(2,1)S(1)}) custom-call(s32[1]{0:T(128)} %bitcast.me_ref, bf16[1024,768]{1,0:T(8,128)(2,1)S(1)} %get-tuple-element.66.h_ref, bf16[1024,768]{1,0:T(8,128)(2,1)S(1)} %copy-done.20, ...), custom_call_target="tpu_custom_call" | custom-call | flops 4831838208 | bytes 15728640 | tf_op jit(solution)/shard_map/pallas_call | solution.py:280
  189.3 43.8 %shard_map.205 = (bf16[1024,768]{1,0:T(8,128)(2,1)S(1)}, bf16[1024,768]{1,0:T(8,128)(2,1)S(1)}, bf16[1024,768]{1,0:T(8,128)(2,1)S(1)}, bf16[1024,768]{1,0:T(8,128)(2,1)S(1)}, f32[2,3,768]{2,1,0:T(4,128)S(1)}) custom-call(bf16[1024,768]{1,0:T(8,128)(2,1)S(1)} %get-tuple-element.68.q_ref, bf16[1024,768]{1,0:T(8,128)(2,1)S(1)} %get-tuple-element.69.k_ref, ...), custom_call_target="tpu_custom_call" | custom-call | flops 20000000000 | bytes 15728640 | tf_op jit(solution)/shard_map/pallas_call | solution.py:364
  233.2 13.7 %shard_map.211 = (bf16[4,2,96,768]{3,2,1,0:T(8,128)(2,1)S(1)}, bf16[4,2,96,768]{3,2,1,0:T(8,128)(2,1)S(1)}, bf16[4,2,96,768]{3,2,1,0:T(8,128)(2,1)S(1)}, bf16[4,2,96,768]{3,2,1,0:T(8,128)(2,1)S(1)}) custom-call(s32[1]{0:T(128)} %bitcast.me_ref, bf16[1024,768]{1,0:T(8,128)(2,1)S(1)} %get-tuple-element.66.h_ref, ...), custom_call_target="tpu_custom_call" | custom-call | flops 4831838208 | bytes 9437184 | tf_op jit(solution)/shard_map/pallas_call | solution.py:407
  251.8 5.5 collective-permute-done.20
  260.6 12.0 %collective-permute-done.29 = bf16[2,2,96,768]{3,2,1,0:T(8,128)(2,1)S(1)} collective-permute-done((bf16[2,2,96,768]{3,2,1,0:T(8,128)(2,1)S(1)}, bf16[2,2,96,768]{3,2,1,0:T(8,128)(2,1)S(1)}, u32[]{:S(2)}, u32[]{:S(2)}) %collective-permute-start.29) | collective-permute-done | bytes 589856 | tf_op jit(solution)/shard_map/ppermute | solution.py:554
  288.4 10.3 %collective-permute-done.34 = bf16[4,96,768]{2,1,0:T(8,128)(2,1)S(1)} collective-permute-done((bf16[4,96,768]{2,1,0:T(8,128)(2,1)S(1)}, bf16[4,96,768]{2,1,0:T(8,128)(2,1)S(1)}, u32[]{:S(2)}, u32[]{:S(2)}) %collective-permute-start.34) | collective-permute-done | bytes 589856 | tf_op jit(solution)/shard_map/ppermute | solution.py:566
  310.6 13.0 %shard_map.209 = (bf16[1024,768]{1,0:T(8,128)(2,1)S(1)}, bf16[1024,768]{1,0:T(8,128)(2,1)S(1)}, f32[1,768]{1,0:T(1,128)S(1)}, bf16[4,1,96,768]{3,2,1,0:T(8,128)(...) custom-call(s32[1]{0:T(128)} %bitcast.me_ref, ...), custom_call_target="tpu_custom_call" | custom-call | flops 4831838208 | bytes 12582912 | tf_op jit(solution)/shard_map/pallas_call | solution.py:206
  327.5 13.1 %shard_map.208 = (bf16[1024,768]{1,0:T(8,128)(2,1)S(1)}, bf16[1024,768]{1,0:T(8,128)(2,1)S(1)}, f32[1,768]{1,0:T(1,128)S(1)}, bf16[4,1,96,768]{3,2,1,0:T(8,128)(...) custom-call(s32[1]{0:T(128)} %bitcast.me_ref, ...), custom_call_target="tpu_custom_call" | custom-call | flops 4831838208 | bytes 12582912 | tf_op jit(solution)/shard_map/pallas_call | solution.py:206
  344.6 13.4 %shard_map.207 = (bf16[1024,768]{1,0:T(8,128)(2,1)S(1)}, bf16[1024,768]{1,0:T(8,128)(2,1)S(1)}, f32[1,768]{1,0:T(1,128)S(1)}, bf16[4,1,96,768]{3,2,1,0:T(8,128)(...) custom-call(s32[1]{0:T(128)} %bitcast.me_ref, ...), custom_call_target="tpu_custom_call" | custom-call | flops 4831838208 | bytes 12582912 | tf_op jit(solution)/shard_map/pallas_call | solution.py:206
  362.2 40.8 %shard_map.210 = (bf16[1024,768]{1,0:T(8,128)(2,1)}, f32[1024,768]{1,0:T(8,128)}, f32[5,768]{1,0:T(8,128)S(1)}) custom-call(s32[1]{0:T(128)} %bitcast.me_ref, bf16[1024,768]{1,0:T(8,128)(2,1)S(1)} %copy-done.6, bf16[1024,768]{1,0:T(8,128)(2,1)S(1)} %copy-done.22, f32[13,768]{1,0:T(8,128)S(1)} %copy-done.14, bf16[1024,768]{1,0:T(8,128)(2,1)} %copy-done.36, ...), custom_call_target="tpu_custom_call" | custom-call | flops 14495514624 | bytes 31457280 | tf_op jit(solution)/shard_map/pallas_call | solution.py:493
  412.8 15.6 %collective-permute-start.70 = (f32[13,768]{1,0:T(8,128)S(1)}, f32[13,768]{1,0:T(8,128)S(1)}, u32[]{:S(2)}, u32[]{:S(2)}) collective-permute-start(f32[13,768]{1,0:T(8,128)S(1)} %add.255), channel_id=1, source_target_pairs={{0,1},{1,0},{2,3},{3,2},{4,5},{5,4},{6,7},{7,6},{8,9},{9,8},{10,11... | collective-permute-start | bytes 119816 | tf_op jit(solution)/shard_map/ppermute | solution.py:554
  467.6 5.0 collective-permute-done.48
  482.6 7.6 %collective-permute-done.43 = bf16[2,96,768]{2,1,0:T(8,128)(2,1)S(1)} collective-permute-done((bf16[2,96,768]{2,1,0:T(8,128)(2,1)S(1)}, bf16[2,96,768]{2,1,0:T(8,128)(2,1)S(1)}, u32[]{:S(2)}, u32[]{:S(2)}) %collective-permute-start.43) | collective-permute-done | bytes 294944 | tf_op jit(solution)/shard_map/ppermute | solution.py:566
  499.3 13.9 %collective-permute-done.45 = bf16[2,96,768]{2,1,0:T(8,128)(2,1)S(1)} collective-permute-done((bf16[2,96,768]{2,1,0:T(8,128)(2,1)S(1)}, bf16[2,96,768]{2,1,0:T(8,128)(2,1)S(1)}, u32[]{:S(2)}, u32[]{:S(2)}) %collective-permute-start.45) | collective-permute-done | bytes 294944 | tf_op jit(solution)/shard_map/ppermute | solution.py:568
  541.2 4.9 shard_map.212
  (391 shorter events, 205.1 us)
Async XLA Ops:
  7.2 300.5 %all-gather.3.cloned.1.call-start = ((), (), s32[]{:S(2)}) async-start(), calls=%async_computation | async-start | bytes 7962624 | tf_op jit(solution)/shard_map/all_gather | solution.py:579
  11.8 25.0 %collective-permute-start.16 = (bf16[6,96,768]{2,1,0:T(8,128)(2,1)S(1)}, bf16[6,96,768]{2,1,0:T(8,128)(2,1)S(1)}, u32[]{:S(2)}, u32[]{:S(2)}) collective-permute-start(bf16[6,96,768]{2,1,0:T(8,128)(2,1)S(1)} %get-tuple-element.79), channel_id=1, source_target_pairs={{0,1},{3,2},{4,5},{7,6},{8,9},{11,10},{12,13},{15,14},{16,17},{19,... | collective-permute-start | bytes 2654216 | tf_op jit(solution)/shard_map/ppermute | solution.py:566
  16.8 31.5 %collective-permute-start = (bf16[4,96,768]{2,1,0:T(8,128)(2,1)S(1)}, bf16[4,96,768]{2,1,0:T(8,128)(2,1)S(1)}, u32[]{:S(2)}, u32[]{:S(2)}) collective-permute-start(bf16[4,96,768]{2,1,0:T(8,128)(2,1)S(1)} %get-tuple-element.67), channel_id=1, source_target_pairs={{0,1},{3,2},{4,5},{7,6},{8,9},{11,10},{12,13},{15,14},{16,17},{19,... | collective-permute-start | bytes 1769480 | tf_op jit(solution)/shard_map/ppermute | solution.py:566
  49.3 45.4 %collective-permute-start.18 = (bf16[6,96,768]{2,1,0:T(8,128)(2,1)S(1)}, bf16[6,96,768]{2,1,0:T(8,128)(2,1)}, u32[]{:S(2)}, u32[]{:S(2)}) collective-permute-start(bf16[6,96,768]{2,1,0:T(8,128)(2,1)S(1)} %add_convert_fusion.2), channel_id=1, source_target_pairs={{1,0},{2,3},{5,4},{6,7},{9,8},{10,11},{13,12},{14,15},{17,16},{18,... | collective-permute-start | bytes 2654216 | tf_op jit(solution)/shard_map/ppermute | solution.py:568
  50.8 40.8 %collective-permute-start.2 = (bf16[4,96,768]{2,1,0:T(8,128)(2,1)S(1)}, bf16[4,96,768]{2,1,0:T(8,128)(2,1)S(1)}, u32[]{:S(2)}, u32[]{:S(2)}) collective-permute-start(bf16[4,96,768]{2,1,0:T(8,128)(2,1)S(1)} %add_convert_fusion.16), channel_id=1, source_target_pairs={{1,0},{2,3},{5,4},{6,7},{9,8},{10,11},{13,12},{14,15},{17,16},{18,... | collective-permute-start | bytes 1769480 | tf_op jit(solution)/shard_map/ppermute | solution.py:568
  52.1 28.9 %collective-permute-start.8 = (bf16[2,96,768]{2,1,0:T(8,128)(2,1)S(1)}, bf16[2,96,768]{2,1,0:T(8,128)(2,1)S(1)}, u32[]{:S(2)}, u32[]{:S(2)}) collective-permute-start(bf16[2,96,768]{2,1,0:T(8,128)(2,1)S(1)} %get-tuple-element.77), channel_id=1, source_target_pairs={{0,1},{3,2},{4,5},{7,6},{8,9},{11,10},{12,13},{15,14},{16,17},{19,... | collective-permute-start | bytes 884744 | tf_op jit(solution)/shard_map/ppermute | solution.py:566
  93.2 19.6 %collective-permute-start.3 = (bf16[4,96,768]{2,1,0:T(8,128)(2,1)S(1)}, bf16[4,96,768]{2,1,0:T(8,128)(2,1)S(1)}, u32[]{:S(2)}, u32[]{:S(2)}) collective-permute-start(bf16[4,96,768]{2,1,0:T(8,128)(2,1)S(1)} %broadcast_select_fusion.2), channel_id=1, source_target_pairs={{0,8},{4,12},{8,0},{12,4},{16,24},{20,28},{24,16},{28,20},{1,9},{5... | collective-permute-start | bytes 1769480 | tf_op jit(solution)/shard_map/ppermute | solution.py:554
  104.6 17.5 %collective-permute-start.6 = (bf16[2,96,768]{2,1,0:T(8,128)(2,1)S(1)}, bf16[2,96,768]{2,1,0:T(8,128)(2,1)S(1)}, u32[]{:S(2)}, u32[]{:S(2)}) collective-permute-start(bf16[2,96,768]{2,1,0:T(8,128)(2,1)S(1)} %slice.247), channel_id=1, source_target_pairs={{0,8},{4,12},{8,0},{12,4},{16,24},{20,28},{24,16},{28,20},{1,9},{5... | collective-permute-start | bytes 884744 | tf_op jit(solution)/shard_map/ppermute | solution.py:554
  123.8 50.9 %collective-permute-start.7 = (bf16[4,4,96,768]{3,2,1,0:T(8,128)(2,1)S(1)}, bf16[4,4,96,768]{3,2,1,0:T(8,128)(2,1)}, u32[]{:S(2)}, u32[]{:S(2)}) collective-permute-start(bf16[4,4,96,768]{3,2,1,0:T(8,128)(2,1)S(1)} %pad_maximum_fusion.rest_0_.rest_8_), channel_id=1, source_target_pairs={{0,4},{4,0},{8,12},{12,8},{16,20},{20,16},{24,28},{28,24},{1,5},{5... | collective-permute-start | bytes 7077896 | tf_op jit(solution)/shard_map/ppermute | solution.py:554
  136.5 23.1 %collective-permute-start.15 = (bf16[4,2,96,768]{3,2,1,0:T(8,128)(2,1)S(1)}, bf16[4,2,96,768]{3,2,1,0:T(8,128)(2,1)}, u32[]{:S(2)}, u32[]{:S(2)}) collective-permute-start(bf16[4,2,96,768]{3,2,1,0:T(8,128)(2,1)S(1)} %pad_maximum_fusion.1.rest_0_.rest_10_), channel_id=1, source_target_pairs={{0,4},{4,0},{8,12},{12,8},{16,20},{20,16},{24,28},{28,24},{1,5},{5... | collective-permute-start | bytes 3538952 | tf_op jit(solution)/shard_map/ppermute | solution.py:554
  174.1 73.6 %collective-permute-start.19 = (bf16[4,1,96,768]{3,2,1,0:T(8,128)(2,1)S(1)}, bf16[4,1,96,768]{3,2,1,0:T(8,128)(2,1)S(1)}, u32[]{:S(2)}, u32[]{:S(2)}) collective-permute-start(bf16[4,1,96,768]{3,2,1,0:T(8,128)(2,1)S(1)} %get-tuple-element.90), channel_id=1, source_target_pairs={{0,4},{4,0},{8,12},{12,8},{16,20},{20,16},{24,28},{28,24},{1,5},{5... | collective-permute-start | bytes 1769480 | tf_op jit(solution)/shard_map/ppermute | solution.py:554
  258.0 28.9 %collective-permute-start.21 = (bf16[1,96,768]{2,1,0:T(8,128)(2,1)S(1)}, bf16[1,96,768]{2,1,0:T(8,128)(2,1)S(1)}, u32[]{:S(2)}, u32[]{:S(2)}) collective-permute-start(bf16[1,96,768]{2,1,0:T(8,128)(2,1)S(1)} %slice_bitcast_fusion.18), channel_id=1, source_target_pairs={{0,16},{4,20},{8,24},{12,28},{16,0},{20,4},{24,8},{28,12},{1,17},{... | collective-permute-start | bytes 442376 | tf_op jit(solution)/shard_map/ppermute | solution.py:554
  259.2 18.3 %collective-permute-start.32 = (bf16[2,2,96,768]{3,2,1,0:T(8,128)(2,1)S(1)}, bf16[2,2,96,768]{3,2,1,0:T(8,128)(2,1)S(1)}, u32[]{:S(2)}, u32[]{:S(2)}) collective-permute-start(bf16[2,2,96,768]{3,2,1,0:T(8,128)(2,1)S(1)} %slice.263), channel_id=1, source_target_pairs={{0,16},{4,20},{8,24},{12,28},{16,0},{20,4},{24,8},{28,12},{1,17},{... | collective-permute-start | bytes 1769480 | tf_op jit(solution)/shard_map/ppermute | solution.py:554
  303.5 102.4 %collective-permute-start.27 = (bf16[2,96,768]{2,1,0:T(8,128)(2,1)}, bf16[2,96,768]{2,1,0:T(8,128)(2,1)}, u32[]{:S(2)}, u32[]{:S(2)}) collective-permute-start(bf16[2,96,768]{2,1,0:T(8,128)(2,1)} %add_convert_fusion.30), channel_id=1, source_target_pairs={{1,0},{2,3},{5,4},{6,7},{9,8},{10,11},{13,12},{14,15},{17,16},{18,... | collective-permute-start | bytes 884744 | tf_op jit(solution)/shard_map/ppermute | solution.py:568
  306.4 103.1 %collective-permute-start.36 = (bf16[4,96,768]{2,1,0:T(8,128)(2,1)}, bf16[4,96,768]{2,1,0:T(8,128)(2,1)}, u32[]{:S(2)}, u32[]{:S(2)}) collective-permute-start(bf16[4,96,768]{2,1,0:T(8,128)(2,1)} %add_convert_fusion.10), channel_id=1, source_target_pairs={{1,0},{2,3},{5,4},{6,7},{9,8},{10,11},{13,12},{14,15},{17,16},{18,... | collective-permute-start | bytes 1769480 | tf_op jit(solution)/shard_map/ppermute | solution.py:568
  410.7 28.5 %collective-permute-start.55 = (bf16[4,1,96,768]{3,2,1,0:T(8,128)(2,1)}, bf16[4,1,96,768]{3,2,1,0:T(8,128)(2,1)}, u32[]{:S(2)}, u32[]{:S(2)}) collective-permute-start(bf16[4,1,96,768]{3,2,1,0:T(8,128)(2,1)} %copy-done.29), channel_id=1, source_target_pairs={{0,4},{4,0},{8,12},{12,8},{16,20},{20,16},{24,28},{28,24},{1,5},{5... | collective-permute-start | bytes 1769480 | tf_op jit(solution)/shard_map/ppermute | solution.py:554
  412.8 17.7 %collective-permute-start.70 = (f32[13,768]{1,0:T(8,128)S(1)}, f32[13,768]{1,0:T(8,128)S(1)}, u32[]{:S(2)}, u32[]{:S(2)}) collective-permute-start(f32[13,768]{1,0:T(8,128)S(1)} %add.255), channel_id=1, source_target_pairs={{0,1},{1,0},{2,3},{3,2},{4,5},{5,4},{6,7},{7,6},{8,9},{9,8},{10,11... | collective-permute-start | bytes 119816 | tf_op jit(solution)/shard_map/ppermute | solution.py:554
  447.2 16.4 %collective-permute-start.38 = (bf16[2,1,96,768]{3,2,1,0:T(8,128)(2,1)S(1)}, bf16[2,1,96,768]{3,2,1,0:T(8,128)(2,1)S(1)}, u32[]{:S(2)}, u32[]{:S(2)}) collective-permute-start(bf16[2,1,96,768]{3,2,1,0:T(8,128)(2,1)S(1)} %slice.267), channel_id=1, source_target_pairs={{0,8},{4,12},{8,0},{12,4},{16,24},{20,28},{24,16},{28,20},{1,9},{5... | collective-permute-start | bytes 884744 | tf_op jit(solution)/shard_map/ppermute | solution.py:554
  453.7 27.4 %collective-permute-start.57 = (bf16[1,96,768]{2,1,0:T(8,128)(2,1)S(1)}, bf16[1,96,768]{2,1,0:T(8,128)(2,1)S(1)}, u32[]{:S(2)}, u32[]{:S(2)}) collective-permute-start(bf16[1,96,768]{2,1,0:T(8,128)(2,1)S(1)} %slice_bitcast_fusion.6), channel_id=1, source_target_pairs={{0,16},{4,20},{8,24},{12,28},{16,0},{20,4},{24,8},{28,12},{1,17},{... | collective-permute-start | bytes 442376 | tf_op jit(solution)/shard_map/ppermute | solution.py:554
  457.3 23.9 %collective-permute-start.60 = (bf16[1,96,768]{2,1,0:T(8,128)(2,1)S(1)}, bf16[1,96,768]{2,1,0:T(8,128)(2,1)S(1)}, u32[]{:S(2)}, u32[]{:S(2)}) collective-permute-start(bf16[1,96,768]{2,1,0:T(8,128)(2,1)S(1)} %slice_bitcast_fusion.4), channel_id=1, source_target_pairs={{0,8},{4,12},{8,0},{12,4},{16,24},{20,28},{24,16},{28,20},{1,9},{5... | collective-permute-start | bytes 442376 | tf_op jit(solution)/shard_map/ppermute | solution.py:554
  473.5 17.5 %collective-permute-start.52 = (bf16[2,96,768]{2,1,0:T(8,128)(2,1)S(1)}, bf16[2,96,768]{2,1,0:T(8,128)(2,1)S(1)}, u32[]{:S(2)}, u32[]{:S(2)}) collective-permute-start(bf16[2,96,768]{2,1,0:T(8,128)(2,1)S(1)} %pad_maximum_fusion.6), channel_id=1, source_target_pairs={{0,1},{3,2},{4,5},{7,6},{8,9},{11,10},{12,13},{15,14},{16,17},{19,... | collective-permute-start | bytes 884744 | tf_op jit(solution)/shard_map/ppermute | solution.py:566
  494.5 18.7 %collective-permute-start.45 = (bf16[2,96,768]{2,1,0:T(8,128)(2,1)S(1)}, bf16[2,96,768]{2,1,0:T(8,128)(2,1)S(1)}, u32[]{:S(2)}, u32[]{:S(2)}) collective-permute-start(bf16[2,96,768]{2,1,0:T(8,128)(2,1)S(1)} %add_convert_fusion.26), channel_id=1, source_target_pairs={{1,0},{2,3},{5,4},{6,7},{9,8},{10,11},{13,12},{14,15},{17,16},{18,... | collective-permute-start | bytes 884744 | tf_op jit(solution)/shard_map/ppermute | solution.py:568
  495.9 20.4 %collective-permute-start.54 = (bf16[2,96,768]{2,1,0:T(8,128)(2,1)S(1)}, bf16[2,96,768]{2,1,0:T(8,128)(2,1)S(1)}, u32[]{:S(2)}, u32[]{:S(2)}) collective-permute-start(bf16[2,96,768]{2,1,0:T(8,128)(2,1)S(1)} %add_convert_fusion.22), channel_id=1, source_target_pairs={{1,0},{2,3},{5,4},{6,7},{9,8},{10,11},{13,12},{14,15},{17,16},{18,... | collective-permute-start | bytes 884744 | tf_op jit(solution)/shard_map/ppermute | solution.py:568
  498.0 21.6 %collective-permute-start.63 = (bf16[2,96,768]{2,1,0:T(8,128)(2,1)}, bf16[2,96,768]{2,1,0:T(8,128)(2,1)}, u32[]{:S(2)}, u32[]{:S(2)}) collective-permute-start(bf16[2,96,768]{2,1,0:T(8,128)(2,1)} %add_convert_fusion.18), channel_id=1, source_target_pairs={{1,0},{2,3},{5,4},{6,7},{9,8},{10,11},{13,12},{14,15},{17,16},{18,... | collective-permute-start | bytes 884744 | tf_op jit(solution)/shard_map/ppermute | solution.py:568
  (110 other events, 1116.8 us)
Sparse Core Ops, SparseCore 0:
  97.1 55.2 all-gather.2
